TPU v7x, 32 devices: a whole 2x2x4 slice. The times are simulated.
32 devices in a mesh: gz: 2 (over core), row: 4 (over y, x), col: 4 (over z).
Axes of the slice: x: 2, y: 2, z: 4, core: 2. Of those that a mesh axis runs over, the one named last changes fastest.
Arguments:
- front_matrix: float32 [4096, 4096], P('row', 'col'), may hold values from -6 to 6
- l_panels: float32 [2, 8, 4, 512, 256], P('gz', None, 'row', 'col'), may hold values from -6 to 6
- l_map: int32 [2, 8, 4, 512], P('gz', None, 'row'), may hold values from 0 to 1024, as said below
- u_panels: float32 [2, 8, 4, 512, 256], P('gz', None, 'col', 'row'), may hold values from -0.375 to 0.375
- u_map: int32 [2, 8, 4, 512], P('gz', None, 'col'), may hold values from 0 to 1024, as said below
Outputs:
- updated_front: float32 [4096, 4096], P('row', 'col')
Inputs may be any that keep to these rules, and one draw needn't show every extreme that they name: l_map[z,h,p,:] lists distinct rows of row block p updated by child h of layer z, used slots first, listed block of 128 rows by block, at most 64 rows to a block; unused slots hold 1024; in every child some row block uses all 512 slots. u_map[z,h,q,:] lists distinct columns of column block q updated by child h of layer z, used slots first, listed block of 128 columns by block, at most 64 to a block; unused slots hold 1024; in every child some column block uses all 512 slots.
All inputs are finite; a program needn't handle non-finite values.
Results may differ from a plain program's by a relative error of at most 0.0001.
Values sent between devices are 32-bit elements; how exact they have to be, the bound alone decides.
No kernel may reach another device: no remote copies, remote signals or barrier semaphores. Data moves between devices by JAX's collectives and lax.ppermute only.
A program may use at most 64 MiB of HBM per device.

v0:
```python
import jax
import jax.numpy as jnp
from jax import lax
from jax.sharding import PartitionSpec as P


def spread_dense(row_panel, row_map, col_dense, row_count):
    targets = jnp.arange(row_count, dtype=jnp.int32)
    narrow = jnp.einsum("hik,hgk->hig", row_panel, col_dense, precision=lax.Precision.HIGHEST)
    row_hot = (row_map[:, :, None] == targets[None, None, :]).astype(jnp.float32)
    return jnp.einsum("hif,hig->fg", row_hot, narrow, precision=lax.Precision.HIGHEST)


def shards(front_matrix, l_panels, l_map, u_panels, u_map):
    row_count, col_count = front_matrix.shape
    row_map = l_map[0, :, 0, :]
    col_map = u_map[0, :, 0, :]
    col_panel = lax.all_gather(u_panels, "row", axis=3, tiled=True)[0, :, 0]
    col_targets = jnp.arange(col_count, dtype=jnp.int32)
    col_hot = (col_map[:, :, None] == col_targets[None, None, :]).astype(jnp.float32)
    col_dense = jnp.einsum("hjg,hjk->hgk", col_hot, col_panel, precision=lax.Precision.HIGHEST)
    row_panel = lax.all_gather(l_panels, "col", axis=3, tiled=True)[0, :, 0]
    update = spread_dense(row_panel, row_map, col_dense, row_count)
    summed = lax.psum(update, "gz")
    return front_matrix - summed


def solution(mesh):
    placed = (
        P("row", "col"),
        P("gz", None, "row", "col", None),
        P("gz", None, "row", None),
        P("gz", None, "col", "row", None),
        P("gz", None, "col", None),
    )
    return jax.shard_map(
        shards, mesh=mesh, in_specs=placed, out_specs=P("row", "col"), check_vma=False
    )
```

profile of v0, /device:TPU:0, one launch (start us, length us, event | category | flops | bytes accessed | tf_op | source)
XLA Modules:
  0.0 234.2 jit_solution(15254661452700204402)
XLA Ops:
  6.5 0.0 all-gather.3.cloned.1.call-start
  6.5 0.7 all-gather.3.cloned.1.call-update
  7.3 0.0 all-gather.5.cloned.1.call-start
  7.3 0.7 all-gather.5.cloned.1.call-update
  8.0 0.0 all-reduce.2.cloned.1.call-start
  8.1 0.7 copy.10
  8.8 0.7 copy.11
  9.5 55.1 %all-gather.3.cloned.1.call-done = f32[1,8,1,512,256]{4,3,2,1,0:T(8,128)} async-done(((f32[1,8,1,128,256]{4,3,2,1,0:T(8,128)}), f32[1,8,1,512,256]{4,3,2,1,0:T(8,128)}) %all-gather.3.cloned.1.call-update) | async-done | bytes 4194320 | tf_op jit(solution)/shard_map/all_gather | solution.py:18
  64.6 17.7 %fusion.2 = f32[8,1024,256]{2,1,0:T(8,128)} fusion(s32[8,512]{1,0:T(8,128)S(1)} %bitcast.21, f32[1,8,1,512,256]{4,3,2,1,0:T(8,128)} %all-gather.3.cloned.1.call-done), kind=kOutput, calls=%fused_computation.4 | convolution fusion | flops 12889096192 | bytes 12599296 | tf_op jit(solution)/shard_map/hjg,hjk->hgk/dot_general | solution.py:21
  82.3 64.7 %all-gather.5.cloned.1.call-done = f32[1,8,1,512,256]{4,3,2,1,0:T(8,128)} async-done(((f32[1,8,1,128,256]{4,3,2,1,0:T(8,128)}), f32[1,8,1,512,256]{4,3,2,1,0:T(8,128)}) %all-gather.5.cloned.1.call-update) | async-done | bytes 4194320 | tf_op jit(solution)/shard_map/all_gather | solution.py:22
  147.0 18.5 %fusion.5 = f32[8,1024,512]{1,2,0:T(8,128)S(1)} fusion(f32[8,1024,256]{2,1,0:T(8,128)} %fusion.2, f32[1,8,1,512,256]{4,3,2,1,0:T(8,128)} %all-gather.5.cloned.1.call-done), kind=kOutput, calls=%fused_computation.7 | convolution fusion | flops 12884901888 | bytes 29360128 | tf_op jit(solution)/shard_map/hik,hgk->hig/dot_general | solution.py:9
  165.6 28.2 %fusion.8 = f32[1024,1024]{1,0:T(8,128)} fusion(f32[8,1024,512]{1,2,0:T(8,128)S(1)} %fusion.5, s32[8,512]{1,0:T(8,128)S(1)} %bitcast.20), kind=kOutput, calls=%fused_computation.10 | convolution fusion | flops 51543801856 | bytes 20987904 | tf_op jit(solution)/shard_map/hif,hig->fg/dot_general | solution.py:11
  193.7 0.0 all-reduce.2.cloned.1.call-update
  193.7 27.1 %all-reduce.2.cloned.1.call-done = f32[1024,1024]{1,0:T(8,128)} async-done(((f32[1024,1024]{1,0:T(8,128)}), f32[1024,1024]{1,0:T(8,128)}) %all-reduce.2.cloned.1.call-update) | async-done | bytes 4194320 | tf_op jit(solution)/shard_map/psum | solution.py:24
  220.8 6.8 %sub.3 = f32[1024,1024]{1,0:T(8,128)} subtract(f32[1024,1024]{1,0:T(8,128)} %param.5, f32[1024,1024]{1,0:T(8,128)} %all-reduce.2.cloned.1.call-done) | non-fusion elementwise | flops 1048576 | bytes 12582912 | tf_op jit(solution)/shard_map/sub | solution.py:25
Async XLA Ops:
  6.5 58.1 %all-gather.3.cloned.1.call-start = ((), (), s32[]{:S(2)}) async-start(), calls=%async_computation | async-start | bytes 5242880 | tf_op jit(solution)/shard_map/all_gather | solution.py:18
  7.3 139.8 %all-gather.5.cloned.1.call-start = ((), (), s32[]{:S(2)}) async-start(), calls=%async_computation.1 | async-start | bytes 5242880 | tf_op jit(solution)/shard_map/all_gather | solution.py:22
  8.0 212.8 %all-reduce.2.cloned.1.call-start = ((), (), s32[]{:S(2)}) async-start(), calls=%async_computation.2 | async-start | bytes 8388608 | tf_op jit(solution)/shard_map/psum | solution.py:24
Sparse Core Ops, SparseCore 0:
  9.2 55.3 all-gather.2
  66.2 80.7 all-gather.4
  193.9 26.9 all-reduce.1
where the time goes:
time: 235 us; the launch traced here: 234 us
  waiting for transfers between devices  148 us (63%)
  matrix products  64.4 us (27%)
  between operations  13.1 us (6%)
  other arithmetic  6.85 us (3%)
    all_gather x1, waiting for transfers between devices, shards(): row_panel = lax.all_gather(l_panels, 'col', axis=3, tiled=True)[0, :, 0]  64.7 us
    all_gather x1, waiting for transfers between devices, shards(): col_panel = lax.all_gather(u_panels, 'row', axis=3, tiled=True)[0, :, 0]  55.1 us
    dot_general x1, matrix products, spread_dense(): jnp.einsum('hif,hig->fg', row_hot, narrow, precision=lax.Precision.HIGHEST)  28.2 us
    psum x1, waiting for transfers between devices, shards(): summed = lax.psum(update, 'gz')  27.1 us
    dot_general x1, matrix products, spread_dense(): jnp.einsum('hik,hgk->hig', row_panel, col_dense, precision=lax.Precision....  18.5 us
    dot_general x1, matrix products, shards(): jnp.einsum('hjg,hjk->hgk', col_hot, col_panel, precision=lax.Precision.HI...  17.7 us
    sub x1, other arithmetic, shards(): return front_matrix - summed  6.85 us
  transfers between devices with their start and end apart: 3, of which 3 were waited for; matrix products, arithmetic and copies ran while one was open for 8% of the time, Pallas kernels for 0%

commit v1 on v0

--- a/solution.py
+++ b/solution.py
@@ -1,7 +1,15 @@
+import functools
+
 import jax
 import jax.numpy as jnp
 from jax import lax
+from jax.experimental import pallas as pl
+from jax.experimental.pallas import tpu as pltpu
 from jax.sharding import PartitionSpec as P
+
+F32 = jnp.float32
+BF16 = jnp.bfloat16
+VMEM_LIMIT = 48 * 1024 * 1024
 
 
 def spread_dense(row_panel, row_map, col_dense, row_count):
@@ -11,7 +19,7 @@
     return jnp.einsum("hif,hig->fg", row_hot, narrow, precision=lax.Precision.HIGHEST)
 
 
-def shards(front_matrix, l_panels, l_map, u_panels, u_map):
+def any_mesh(front_matrix, l_panels, l_map, u_panels, u_map):
     row_count, col_count = front_matrix.shape
     row_map = l_map[0, :, 0, :]
     col_map = u_map[0, :, 0, :]
@@ -25,6 +33,176 @@
     return front_matrix - summed
 
 
+def split(x):
+    high = x.astype(BF16)
+    return high, (x - high.astype(F32)).astype(BF16)
+
+
+def dot(a, b):
+    return jnp.dot(a, b, preferred_element_type=F32)
+
+
+def dot_t(a, b):
+    return lax.dot_general(a, b, (((1,), (1,)), ((), ())), preferred_element_type=F32)
+
+
+def one_hot(slots, first, count):
+    rows = lax.broadcasted_iota(jnp.int32, (count, slots.shape[-1]), 0) + first
+    return jnp.where(rows == slots, 1.0, 0.0).astype(BF16)
+
+
+def densify_kernel(map_ref, own, by_x, by_y, by_xy_a, by_xy_b, high_ref, low_ref):
+    here = lax.axis_index("row")
+    child = pl.program_id(0)
+    far = jnp.where(child < pl.num_programs(0) // 2, by_xy_a[0], by_xy_b[0])
+    panel = jnp.concatenate([own[0], by_x[0], by_y[0], far], axis=0)
+    count = high_ref.shape[1]
+    hot = jnp.concatenate(
+        [one_hot(map_ref[0, pl.ds(here ^ part, 1), :], 0, count) for part in range(4)], axis=1
+    )
+    high, low = split(panel)
+    high_ref[0] = dot(hot, high).astype(BF16)
+    low_ref[0] = dot(hot, low).astype(BF16)
+
+
+def densify(col_map, own, by_x, by_y, by_xy_a, by_xy_b, col_count):
+    children, part, depth = own.shape
+    half = children // 2
+    block = (1, part, depth)
+    whole = pl.BlockSpec(block, lambda h: (h, 0, 0))
+    dense = jax.ShapeDtypeStruct((children, col_count, depth), BF16)
+    dense_spec = pl.BlockSpec((1, col_count, depth), lambda h: (h, 0, 0))
+    return pl.pallas_call(
+        densify_kernel,
+        grid=(children,),
+        in_specs=[
+            pl.BlockSpec((1,) + col_map.shape[1:], lambda h: (h, 0, 0)),
+            whole,
+            whole,
+            whole,
+            pl.BlockSpec(block, lambda h: (jnp.minimum(h, half - 1), 0, 0)),
+            pl.BlockSpec(block, lambda h: (jnp.maximum(h - half, 0), 0, 0)),
+        ],
+        out_specs=[dense_spec, dense_spec],
+        out_shape=[dense, dense],
+        compiler_params=pltpu.CompilerParams(vmem_limit_bytes=VMEM_LIMIT),
+        cost_estimate=pl.CostEstimate(
+            flops=4 * children * 4 * part * col_count * depth,
+            bytes_accessed=children * depth * (16 * part + 4 * col_count),
+            transcendentals=0,
+        ),
+    )(col_map, own, by_x, by_y, by_xy_a, by_xy_b)
+
+
+def chunk_ids(here):
+    end = (here == 0) | (here == 3)
+    low = here < 2
+    return here, here ^ 1, jnp.where(low, 2, 1), jnp.where(low, 3, 0)
+
+
+def update_kernel(map_ref, own, pair, mid_a, mid_b, far_a, far_b, uh, ul, out_ref, lh, ll, hot, nh, nl):
+    ids = chunk_ids(lax.axis_index("col"))
+    children, part, depth = own.shape
+    chunks = len(ids)
+    rows = out_ref.shape[0]
+    step = rows // chunks
+
+    @pl.when(pl.program_id(0) == 0)
+    def _():
+        def prepare(h, carry):
+            at = pl.ds(pl.multiple_of(h * part, part), part)
+            panels = (own[h], pair[h], mid_a[h] + mid_b[h], far_a[h] + far_b[h])
+            for c in range(chunks):
+                high, low = split(panels[c])
+                lh[h, c * part : (c + 1) * part, :] = high
+                ll[h, c * part : (c + 1) * part, :] = low
+                hot[c, :, at] = one_hot(map_ref[h, pl.ds(ids[c], 1), :], 0, rows)
+            return carry
+
+        lax.fori_loop(0, children, prepare, 0)
+
+    def narrow(h, carry):
+        at = pl.ds(pl.multiple_of(h * part, part), part)
+        n = dot_t(lh[h], uh[h]) + dot_t(lh[h], ul[h]) + dot_t(ll[h], uh[h])
+        high, low = split(n)
+        for c in range(chunks):
+            nh[c, at, :] = high[c * part : (c + 1) * part]
+            nl[c, at, :] = low[c * part : (c + 1) * part]
+        return carry
+
+    lax.fori_loop(0, children, narrow, 0)
+    out_ref[...] = jnp.zeros_like(out_ref)
+    for c in range(chunks):
+
+        def place(j, carry, c=c):
+            at = pl.ds(pl.multiple_of(j * step, step), step)
+            a = hot[c, at, :]
+            out_ref[at, :] += dot(a, nh[c]) + dot(a, nl[c])
+            return carry
+
+        lax.fori_loop(ids[c], chunks, place, 0)
+
+
+def update_of(row_map, panels, dense, row_count):
+    own = panels[0]
+    children, part, depth = own.shape
+    col_count = dense[0].shape[1]
+    wide = 256
+    chunks = 4
+    whole = pl.BlockSpec(own.shape, lambda g: (0, 0, 0))
+    dense_spec = pl.BlockSpec((children, wide, depth), lambda g: (0, g, 0))
+    slots = children * part
+    return pl.pallas_call(
+        update_kernel,
+        grid=(col_count // wide,),
+        in_specs=[pl.BlockSpec(row_map.shape, lambda g: (0, 0, 0))] + [whole] * 6 + [dense_spec] * 2,
+        out_specs=pl.BlockSpec((row_count, wide), lambda g: (0, g)),
+        out_shape=jax.ShapeDtypeStruct((row_count, col_count), F32),
+        scratch_shapes=[
+            pltpu.VMEM((children, chunks * part, depth), BF16),
+            pltpu.VMEM((children, chunks * part, depth), BF16),
+            pltpu.VMEM((chunks, row_count, slots), BF16),
+            pltpu.VMEM((chunks, slots, wide), BF16),
+            pltpu.VMEM((chunks, slots, wide), BF16),
+        ],
+        compiler_params=pltpu.CompilerParams(vmem_limit_bytes=VMEM_LIMIT),
+        cost_estimate=pl.CostEstimate(
+            flops=6 * chunks * slots * col_count * depth + 3 * chunks * slots * row_count * col_count,
+            bytes_accessed=4 * row_count * col_count + 4 * children * col_count * depth,
+            transcendentals=0,
+        ),
+    )(row_map, *panels, *dense)
+
+
+ENDS = [(0, 1), (1, 0), (2, 3), (3, 2)]
+MIDDLE = [(1, 2), (2, 1)]
+OUTWARD = [(1, 0), (2, 3)]
+SWAP_X = [(0, 1), (1, 0), (2, 3), (3, 2)]
+SWAP_Y = [(0, 2), (2, 0), (1, 3), (3, 1)]
+
+
+def four_by_four(front_matrix, l_panels, l_map, u_panels, u_map):
+    row_count, col_count = front_matrix.shape
+    l_own = l_panels[0, :, 0]
+    u_own = u_panels[0, :, 0]
+    half = u_own.shape[0] // 2
+    row_map = l_map.reshape(l_own.shape[0], 4, -1)
+    col_map = u_map.reshape(u_own.shape[0], 4, -1)
+    pair = lax.ppermute(l_own, "col", ENDS)
+    mid_b = lax.ppermute(l_own, "col", MIDDLE)
+    by_x = lax.ppermute(u_own, "row", SWAP_X)
+    by_y = lax.ppermute(u_own, "row", SWAP_Y)
+    mid_a = lax.ppermute(mid_b, "col", OUTWARD)
+    far_b = lax.ppermute(pair, "col", MIDDLE)
+    far_a = lax.ppermute(far_b, "col", OUTWARD)
+    by_xy_a = lax.ppermute(by_x[:half], "row", SWAP_Y)
+    by_xy_b = lax.ppermute(by_y[half:], "row", SWAP_X)
+    dense = densify(col_map, u_own, by_x, by_y, by_xy_a, by_xy_b, col_count)
+    mine = update_of(row_map, (l_own, pair, mid_a, mid_b, far_a, far_b), dense, row_count)
+    other = lax.ppermute(mine, "gz", [(0, 1), (1, 0)])
+    return front_matrix - (mine + other)
+
+
 def solution(mesh):
     placed = (
         P("row", "col"),
@@ -33,6 +211,11 @@
         P("gz", None, "col", "row", None),
         P("gz", None, "col", None),
     )
+    square = mesh.shape["row"] == 4 and mesh.shape["col"] == 4
     return jax.shard_map(
-        shards, mesh=mesh, in_specs=placed, out_specs=P("row", "col"), check_vma=False
+        four_by_four if square else any_mesh,
+        mesh=mesh,
+        in_specs=placed,
+        out_specs=P("row", "col"),
+        check_vma=False,
     )

time: 235 us -> 130 us (0.55)
  waiting for transfers between devices: 148 us -> 64.4 us
  matrix products: 64.4 us -> 0 us
  Pallas kernels: 0 us -> 44.7 us
  starting transfers between devices: 0.08 us -> 13.3 us
  between operations: 13.1 us -> 0.07 us
    all_gather x2 -> x0, waiting for transfers between devices: 120 us -> none  [the longest x1 64.7 us: shards(): row_panel = lax.all_gather(l_panels, 'col', axis=3, tiled=True)[0, :, 0]]
    ppermute x0 -> x10, waiting for transfers between devices: none -> 64.4 us  [the longest x1 22.6 us: four_by_four(): pair = lax.ppermute(l_own, 'col', ENDS)]
    dot_general x3 -> x0, matrix products: 64.4 us -> none  [the longest x1 28.2 us: spread_dense(): jnp.einsum('hif,hig->fg', row_hot, narrow, precision=lax.Precision.HIGHEST)]
    pallas_call x0 -> x2, Pallas kernels: none -> 44.7 us  [the longest x1 37.2 us: update_of(): pl.pallas_call(update_kernel, grid=(col_count // wide,), in_specs=[pl.Blo...]
    psum x1 -> x0, waiting for transfers between devices: 27.1 us -> none  [shards(): summed = lax.psum(update, 'gz')]
    ppermute x0 -> x10, starting transfers between devices: none -> 13.3 us  [the longest x1 3.02 us: four_by_four(): pair = lax.ppermute(l_own, 'col', ENDS)]
  transfers between devices with their start and end apart: 3 -> 10, of which waited for: 3 -> 6; matrix products, arithmetic and copies ran while one was open for 8% -> 0% of each run, Pallas kernels for 0% -> 6%
where the time goes in v1:
time: 130 us
  waiting for transfers between devices  64.4 us (50%)
  Pallas kernels  44.7 us (34%)
  starting transfers between devices  13.3 us (10%)
  other arithmetic  5.68 us (4%)
  local copies, waits for them, and re-layouts  2.03 us (2%)
    pallas_call x1, Pallas kernels, update_of(): pl.pallas_call(update_kernel, grid=(col_count // wide,), in_specs=[pl.Blo...  37.2 us
    ppermute x1, waiting for transfers between devices, four_by_four(): pair = lax.ppermute(l_own, 'col', ENDS)  22.6 us
    ppermute x1, waiting for transfers between devices, four_by_four(): by_y = lax.ppermute(u_own, 'row', SWAP_Y)  18.8 us
    ppermute x1, waiting for transfers between devices, four_by_four(): by_xy_b = lax.ppermute(by_y[half:], 'row', SWAP_X)  9.25 us
    pallas_call x1, Pallas kernels, densify(): pl.pallas_call(densify_kernel, grid=(children,), in_specs=[pl.BlockSpec((...  7.47 us
    ppermute x1, waiting for transfers between devices, four_by_four(): other = lax.ppermute(mine, 'gz', [(0, 1), (1, 0)])  7.37 us
    sub x1, other arithmetic, four_by_four(): return front_matrix - (mine + other)  5.68 us
    ppermute x1, waiting for transfers between devices, four_by_four(): far_a = lax.ppermute(far_b, 'col', OUTWARD)  5.58 us
  transfers between devices with their start and end apart: 10, of which 6 were waited for; matrix products, arithmetic and copies ran while one was open for 0% of the time, Pallas kernels for 6%

profile of v1, /device:TPU:0, one launch (start us, length us, event | category | flops | bytes accessed | tf_op | source)
XLA Modules:
  0.0 130.1 jit_solution(17549918981011178893)
XLA Ops:
  0.0 3.0 %collective-permute-start = (f32[8,128,256]{2,1,0:T(8,128)}, f32[8,128,256]{2,1,0:T(8,128)S(1)}, u32[]{:S(2)}, u32[]{:S(2)}) collective-permute-start(f32[8,128,256]{2,1,0:T(8,128)} %bitcast.7), channel_id=1, source_target_pairs={{0,1},{1,0},{2,3},{3,2},{4,5},{5,4},{6,7},{7,6},{8,9},{9,8},{10,11... | collective-permute-start | bytes 3145736 | tf_op jit(solution)/shard_map/ppermute | solution.py:191
  3.0 0.7 collective-permute-start.1
  3.7 22.6 %collective-permute-done.pair = f32[8,128,256]{2,1,0:T(8,128)S(1)} collective-permute-done((f32[8,128,256]{2,1,0:T(8,128)}, f32[8,128,256]{2,1,0:T(8,128)S(1)}, u32[]{:S(2)}, u32[]{:S(2)}) %collective-permute-start) | collective-permute-done | bytes 1048608 | tf_op jit(solution)/shard_map/ppermute | solution.py:191
  26.4 0.7 collective-permute-start.3
  27.1 1.8 %collective-permute-start.6 = (f32[8,128,256]{2,1,0:T(8,128)}, f32[8,128,256]{2,1,0:T(8,128)S(1)}, u32[]{:S(2)}, u32[]{:S(2)}) collective-permute-start(f32[8,128,256]{2,1,0:T(8,128)} %bitcast.4), channel_id=1, source_target_pairs={{0,8},{8,0},{4,12},{12,4},{1,9},{9,1},{5,13},{13,5},{2,10},{10,2},... | collective-permute-start | bytes 3145736 | tf_op jit(solution)/shard_map/ppermute | solution.py:194
  28.9 1.5 %collective-permute-start.5 = (f32[8,128,256]{2,1,0:T(8,128)}, f32[8,128,256]{2,1,0:T(8,128)S(1)}, u32[]{:S(2)}, u32[]{:S(2)}) collective-permute-start(f32[8,128,256]{2,1,0:T(8,128)} %bitcast.5), channel_id=1, source_target_pairs={{0,4},{4,0},{8,12},{12,8},{1,5},{5,1},{9,13},{13,9},{2,6},{6,2},{1... | collective-permute-start | bytes 3145736 | tf_op jit(solution)/shard_map/ppermute | solution.py:193
  30.4 0.0 collective-permute-done.1.mid_b
  30.4 1.3 collective-permute-start.2
  31.7 0.0 collective-permute-done.3.far_b
  31.7 0.0 copy-start.5
  31.7 1.3 collective-permute-start.4
  33.0 18.8 %collective-permute-done.6.by_y = f32[8,128,256]{2,1,0:T(8,128)S(1)} collective-permute-done((f32[8,128,256]{2,1,0:T(8,128)}, f32[8,128,256]{2,1,0:T(8,128)S(1)}, u32[]{:S(2)}, u32[]{:S(2)}) %collective-permute-start.6) | collective-permute-done | bytes 1048608 | tf_op jit(solution)/shard_map/ppermute | solution.py:194
  51.8 1.4 %collective-permute-start.8 = (f32[4,128,256]{2,1,0:T(8,128)S(1)}, f32[4,128,256]{2,1,0:T(8,128)S(1)}, u32[]{:S(2)}, u32[]{:S(2)}) collective-permute-start(f32[4,128,256]{2,1,0:T(8,128)S(1)} %slice.9), channel_id=1, source_target_pairs={{0,4},{4,0},{8,12},{12,8},{1,5},{5,1},{9,13},{13,9},{2,6},{6,2},{1... | collective-permute-start | bytes 1572872 | tf_op jit(solution)/shard_map/ppermute | solution.py:199
  53.2 0.0 collective-permute-done.5.by_x
  53.2 1.6 %collective-permute-start.7 = (f32[4,128,256]{2,1,0:T(8,128)S(1)}, f32[4,128,256]{2,1,0:T(8,128)S(1)}, u32[]{:S(2)}, u32[]{:S(2)}) collective-permute-start(f32[4,128,256]{2,1,0:T(8,128)S(1)} %slice.8), channel_id=1, source_target_pairs={{0,8},{8,0},{4,12},{12,4},{1,9},{9,1},{5,13},{13,5},{2,10},{10,2},... | collective-permute-start | bytes 1572872 | tf_op jit(solution)/shard_map/ppermute | solution.py:198
  54.8 9.3 %collective-permute-done.8.by_xy_b = f32[4,128,256]{2,1,0:T(8,128)S(1)} collective-permute-done((f32[4,128,256]{2,1,0:T(8,128)S(1)}, f32[4,128,256]{2,1,0:T(8,128)S(1)}, u32[]{:S(2)}, u32[]{:S(2)}) %collective-permute-start.8) | collective-permute-done | bytes 524320 | tf_op jit(solution)/shard_map/ppermute | solution.py:199
  64.1 0.8 collective-permute-done.7.by_xy_a
  64.9 0.0 copy-start
  64.9 1.2 copy-done
  66.1 0.0 copy-start.2
  66.1 0.7 copy-done.2
  66.8 7.5 %shard_map.55 = (bf16[8,1024,256]{2,1,0:T(8,128)(2,1)}, bf16[8,1024,256]{2,1,0:T(8,128)(2,1)}) custom-call(s32[8,4,128]{2,1,0:T(4,128)S(1)} %bitcast.10, f32[8,128,256]{2,1,0:T(8,128)S(1)} %bitcast.6, f32[8,128,256]{2,1,0:T(8,128)S(1)} %collective-permute-done.5.by_x, f32[8,128,256]{2,1,0:T(8,128)S(1)} %collective-permute-done.6.by_y, ...), custom_call_target="tpu_custom_call" | custom-call | flops 4294967296 | bytes 12582912 | tf_op jit(solution)/shard_map/pallas_call | solution.py:75
  74.3 0.0 copy-done.5
  74.3 0.0 collective-permute-done.2.mid_a
  74.3 5.6 %collective-permute-done.4.far_a = f32[8,128,256]{2,1,0:T(8,128)S(1)} collective-permute-done((f32[8,128,256]{2,1,0:T(8,128)S(1)}, f32[8,128,256]{2,1,0:T(8,128)S(1)}, u32[]{:S(2)}, u32[]{:S(2)}) %collective-permute-start.4) | collective-permute-done | bytes 1048608 | tf_op jit(solution)/shard_map/ppermute | solution.py:197
  79.9 0.0 copy-done.1
  79.9 0.0 copy-done.3
  79.9 37.2 %shard_map.56 = f32[1024,1024]{1,0:T(8,128)} custom-call(s32[8,4,128]{2,1,0:T(4,128)S(1)} %bitcast.11, f32[8,128,256]{2,1,0:T(8,128)S(1)} %bitcast.9, f32[8,128,256]{2,1,0:T(8,128)S(1)} %collective-permute-done.pair, f32[8,128,256]{2,1,0:T(8,128)S(1)} %collective-permute-done.2.mid_a, f32[8,128,256]{2,1,0:T(8,128)S(1)} %collective-permute-done.1.mid_b, ...), custom_call_target="tpu_custom_call" | custom-call | flops 19327352832 | bytes 12582912 | tf_op jit(solution)/shard_map/pallas_call | solution.py:155
  117.1 0.0 collective-permute-start.9
  117.1 7.4 %collective-permute-done.9 = f32[1024,1024]{1,0:T(8,128)S(1)} collective-permute-done((f32[1024,1024]{1,0:T(8,128)}, f32[1024,1024]{1,0:T(8,128)S(1)}, u32[]{:S(2)}, u32[]{:S(2)}) %collective-permute-start.9) | collective-permute-done | bytes 4194336 | tf_op jit(solution)/shard_map/ppermute | solution.py:202
  124.5 0.0 copy-done.4
  124.5 5.7 %add_subtract_fusion = f32[1024,1024]{1,0:T(8,128)} fusion(f32[1024,1024]{1,0:T(8,128)S(1)} %copy-done.4, f32[1024,1024]{1,0:T(8,128)} %shard_map.56, f32[1024,1024]{1,0:T(8,128)S(1)} %collective-permute-done.9), kind=kLoop, calls=%fused_computation | loop fusion | flops 2097152 | bytes 16777216 | tf_op jit(solution)/shard_map/sub | solution.py:203
  (5 shorter events, 0.1 us)
Async XLA Ops:
  0.0 26.4 %collective-permute-start = (f32[8,128,256]{2,1,0:T(8,128)}, f32[8,128,256]{2,1,0:T(8,128)S(1)}, u32[]{:S(2)}, u32[]{:S(2)}) collective-permute-start(f32[8,128,256]{2,1,0:T(8,128)} %bitcast.7), channel_id=1, source_target_pairs={{0,1},{1,0},{2,3},{3,2},{4,5},{5,4},{6,7},{7,6},{8,9},{9,8},{10,11... | collective-permute-start | bytes 3145736 | tf_op jit(solution)/shard_map/ppermute | solution.py:191
  3.0 27.3 %collective-permute-start.1 = (f32[8,128,256]{2,1,0:T(8,128)}, f32[8,128,256]{2,1,0:T(8,128)S(1)}, u32[]{:S(2)}, u32[]{:S(2)}) collective-permute-start(f32[8,128,256]{2,1,0:T(8,128)} %bitcast.8), channel_id=1, source_target_pairs={{1,2},{2,1},{5,6},{6,5},{9,10},{10,9},{13,14},{14,13},{17,18},{18,... | collective-permute-start | bytes 3145736 | tf_op jit(solution)/shard_map/ppermute | solution.py:192
  26.4 5.3 %collective-permute-start.3 = (f32[8,128,256]{2,1,0:T(8,128)S(1)}, f32[8,128,256]{2,1,0:T(8,128)S(1)}, u32[]{:S(2)}, u32[]{:S(2)}) collective-permute-start(f32[8,128,256]{2,1,0:T(8,128)S(1)} %collective-permute-done.pair), channel_id=1, source_target_pairs={{1,2},{2,1},{5,6},{6,5},{9,10},{10,9},{13,14},{14,13},{17,18},{18,... | collective-permute-start | bytes 3145736 | tf_op jit(solution)/shard_map/ppermute | solution.py:196
  27.1 24.6 %collective-permute-start.6 = (f32[8,128,256]{2,1,0:T(8,128)}, f32[8,128,256]{2,1,0:T(8,128)S(1)}, u32[]{:S(2)}, u32[]{:S(2)}) collective-permute-start(f32[8,128,256]{2,1,0:T(8,128)} %bitcast.4), channel_id=1, source_target_pairs={{0,8},{8,0},{4,12},{12,4},{1,9},{9,1},{5,13},{13,5},{2,10},{10,2},... | collective-permute-start | bytes 3145736 | tf_op jit(solution)/shard_map/ppermute | solution.py:194
  28.9 24.3 %collective-permute-start.5 = (f32[8,128,256]{2,1,0:T(8,128)}, f32[8,128,256]{2,1,0:T(8,128)S(1)}, u32[]{:S(2)}, u32[]{:S(2)}) collective-permute-start(f32[8,128,256]{2,1,0:T(8,128)} %bitcast.5), channel_id=1, source_target_pairs={{0,4},{4,0},{8,12},{12,8},{1,5},{5,1},{9,13},{13,9},{2,6},{6,2},{1... | collective-permute-start | bytes 3145736 | tf_op jit(solution)/shard_map/ppermute | solution.py:193
  30.4 43.9 %collective-permute-start.2 = (f32[8,128,256]{2,1,0:T(8,128)S(1)}, f32[8,128,256]{2,1,0:T(8,128)S(1)}, u32[]{:S(2)}, u32[]{:S(2)}) collective-permute-start(f32[8,128,256]{2,1,0:T(8,128)S(1)} %collective-permute-done.1.mid_b), channel_id=1, source_target_pairs={{1,0},{2,3},{5,4},{6,7},{9,8},{10,11},{13,12},{14,15},{17,16},{18,... | collective-permute-start | bytes 3145736 | tf_op jit(solution)/shard_map/ppermute | solution.py:195
  31.7 42.6 %copy-start.5 = (f32[8,128,256]{2,1,0:T(8,128)}, f32[8,128,256]{2,1,0:T(8,128)S(1)}, u32[]{:S(2)}) copy-start(f32[8,128,256]{2,1,0:T(8,128)S(1)} %collective-permute-done.3.far_b) | copy-start | bytes 3145732
  31.7 48.2 %collective-permute-start.4 = (f32[8,128,256]{2,1,0:T(8,128)S(1)}, f32[8,128,256]{2,1,0:T(8,128)S(1)}, u32[]{:S(2)}, u32[]{:S(2)}) collective-permute-start(f32[8,128,256]{2,1,0:T(8,128)S(1)} %collective-permute-done.3.far_b), channel_id=1, source_target_pairs={{1,0},{2,3},{5,4},{6,7},{9,8},{10,11},{13,12},{14,15},{17,16},{18,... | collective-permute-start | bytes 3145736 | tf_op jit(solution)/shard_map/ppermute | solution.py:197
  51.8 12.3 %collective-permute-start.8 = (f32[4,128,256]{2,1,0:T(8,128)S(1)}, f32[4,128,256]{2,1,0:T(8,128)S(1)}, u32[]{:S(2)}, u32[]{:S(2)}) collective-permute-start(f32[4,128,256]{2,1,0:T(8,128)S(1)} %slice.9), channel_id=1, source_target_pairs={{0,4},{4,0},{8,12},{12,8},{1,5},{5,1},{9,13},{13,9},{2,6},{6,2},{1... | collective-permute-start | bytes 1572872 | tf_op jit(solution)/shard_map/ppermute | solution.py:199
  53.2 11.7 %collective-permute-start.7 = (f32[4,128,256]{2,1,0:T(8,128)S(1)}, f32[4,128,256]{2,1,0:T(8,128)S(1)}, u32[]{:S(2)}, u32[]{:S(2)}) collective-permute-start(f32[4,128,256]{2,1,0:T(8,128)S(1)} %slice.8), channel_id=1, source_target_pairs={{0,8},{8,0},{4,12},{12,4},{1,9},{9,1},{5,13},{13,5},{2,10},{10,2},... | collective-permute-start | bytes 1572872 | tf_op jit(solution)/shard_map/ppermute | solution.py:198
  64.9 1.2 copy-start
  66.1 0.7 copy-start.2
  66.8 13.1 %copy-start.1 = (f32[1,8,1,128,256]{4,3,2,1,0:T(8,128)S(1)}, f32[1,8,1,128,256]{4,3,2,1,0:T(8,128)}, u32[]{:S(2)}) copy-start(f32[1,8,1,128,256]{4,3,2,1,0:T(8,128)} %param.6) | copy-start | bytes 3145732
  66.8 13.1 %copy-start.3 = (s32[1,8,1,512]{3,2,1,0:T(1,128)S(1)}, s32[1,8,1,512]{3,2,1,0:T(1,128)}, u32[]{:S(2)}) copy-start(s32[1,8,1,512]{3,2,1,0:T(1,128)} %param.7) | copy-start | bytes 49156
  79.9 44.6 %copy-start.4 = (f32[1024,1024]{1,0:T(8,128)S(1)}, f32[1024,1024]{1,0:T(8,128)}, u32[]{:S(2)}) copy-start(f32[1024,1024]{1,0:T(8,128)} %param.5) | copy-start | bytes 12582916
  117.1 7.4 %collective-permute-start.9 = (f32[1024,1024]{1,0:T(8,128)}, f32[1024,1024]{1,0:T(8,128)S(1)}, u32[]{:S(2)}, u32[]{:S(2)}) collective-permute-start(f32[1024,1024]{1,0:T(8,128)} %shard_map.56), channel_id=1, source_target_pairs={{0,16},{16,0},{1,17},{17,1},{2,18},{18,2},{3,19},{19,3},{4,20},{20... | collective-permute-start | bytes 12582920 | tf_op jit(solution)/shard_map/ppermute | solution.py:202

commit v2 on v0

--- a/solution.py
+++ b/solution.py
@@ -1,7 +1,15 @@
+import functools
+
 import jax
 import jax.numpy as jnp
 from jax import lax
+from jax.experimental import pallas as pl
+from jax.experimental.pallas import tpu as pltpu
 from jax.sharding import PartitionSpec as P
+
+F32 = jnp.float32
+BF16 = jnp.bfloat16
+VMEM_ALL = 60 * 1024 * 1024
 
 
 def spread_dense(row_panel, row_map, col_dense, row_count):
@@ -11,7 +19,7 @@
     return jnp.einsum("hif,hig->fg", row_hot, narrow, precision=lax.Precision.HIGHEST)
 
 
-def shards(front_matrix, l_panels, l_map, u_panels, u_map):
+def any_mesh(front_matrix, l_panels, l_map, u_panels, u_map):
     row_count, col_count = front_matrix.shape
     row_map = l_map[0, :, 0, :]
     col_map = u_map[0, :, 0, :]
@@ -25,6 +33,402 @@
     return front_matrix - summed
 
 
+def split(x):
+    high = x.astype(BF16)
+    return high, (x - high.astype(F32)).astype(BF16)
+
+
+def dot(a, b):
+    return jnp.dot(a, b, preferred_element_type=F32)
+
+
+def dot_t(a, b):
+    return lax.dot_general(a, b, (((1,), (1,)), ((), ())), preferred_element_type=F32)
+
+
+def one_hot(slots, first, count):
+    rows = lax.broadcasted_iota(jnp.int32, (count, slots.shape[-1]), 0) + first
+    return jnp.where(rows == slots, 1.0, 0.0).astype(BF16)
+
+
+def chunk_ids(here):
+    low = here < 2
+    return here, here ^ 1, jnp.where(low, 2, 1), jnp.where(low, 3, 0)
+
+
+def dense_columns(slots, panel_ref, count):
+    half = panel_ref.shape[0] // 2
+    top = dot(one_hot(slots[:, :half], 0, count // 2), panel_ref[:half, :])
+    return jnp.concatenate([top, dot(one_hot(slots, count // 2, count // 2), panel_ref[...])], axis=0)
+
+
+def stage_kernel(plan, *refs):
+    n_in, n_out = plan["inputs"], plan["outputs"]
+    bases = [[refs[i] for i in pieces] for pieces in plan["bases"]]
+    hbm_in, hbm_out = refs[:n_in], refs[n_in : n_in + n_out]
+    scratch = refs[n_in + n_out :]
+    held = dict(zip(plan["held"], scratch))
+    acc, slots_ref, high_ref, low_ref = scratch[len(held) : len(held) + 4]
+    n_staged = 2 * plan["emit"] + plan["sums"]
+    staged = scratch[len(held) + 4 : len(held) + 4 + n_staged]
+    extra = scratch[len(held) + 4 + n_staged : -4]
+    panel_ref = scratch[-4]
+    in_sem, base_sem, out_sem = scratch[-3:]
+    ids = chunk_ids(lax.axis_index("col"))
+    here = lax.axis_index("row")
+    layer = lax.axis_index("gz")
+    row_count, cols = acc.shape
+    part, rows = plan["part"], plan["rows"]
+    blocks = row_count // rows
+    first_dense = n_out - n_staged
+
+    def offset(first):
+        return first(layer) if callable(first) else first
+
+    def whole(i):
+        lane = plan["held"].index(i)
+        first, count = plan["range"][i]
+        return pltpu.make_async_copy(hbm_in[i].at[pl.ds(first, count)], held[i], in_sem.at[lane, 0])
+
+    def one(i, child):
+        lane = plan["held"].index(i)
+        first, _ = plan["range"][i]
+        return pltpu.make_async_copy(hbm_in[i].at[first + child], held[i].at[child], in_sem.at[lane, child])
+
+    def base_copy(n, block, piece=0, at_piece=0):
+        at = pl.ds(pl.multiple_of(block * rows, rows), rows)
+        target = acc if n == 0 else extra[n - 1]
+        source = bases[n][piece].at[pl.ds(at_piece * rows, rows)]
+        return pltpu.make_async_copy(source, target.at[at], base_sem.at[n, block])
+
+    def dense_copy(n, child):
+        return pltpu.make_async_copy(
+            staged[n].at[child], hbm_out[first_dense + n].at[child], out_sem.at[1 + n, child]
+        )
+
+    each = blocks // plan["pieces"]
+
+    def out_copy(block, piece):
+        at = pl.ds(pl.multiple_of(block * rows, rows), rows)
+        to = pl.ds(pl.multiple_of((block - piece * each) * rows, rows), rows)
+        return pltpu.make_async_copy(acc.at[at], hbm_out[piece].at[to], out_sem.at[0, block])
+
+    for i in plan["held"]:
+        if i not in plan["single"]:
+            whole(i).start()
+    for group in plan["groups"]:
+        for child in range(group["count"]):
+            for i in group["dense"]:
+                one(i, child).start()
+    for block in range(blocks):
+        for n, pieces in enumerate(bases):
+            per = blocks // len(pieces)
+            base_copy(n, block, block // per, block % per).start()
+    for i in plan["held"]:
+        if i not in plan["single"]:
+            whole(i).wait()
+
+    for group in plan["groups"]:
+
+        def narrow(child, carry, group=group):
+            if "u" in group:
+                panels = [held[i][child] for i in group["u"][:3]]
+                far_a, far_b = (held[i] for i in group["u"][3:])
+                cut = group["cut"]
+                in_a = far_a[jnp.minimum(child, cut - 1)]
+                in_b = far_b[jnp.maximum(child - cut, 0)]
+                panels.append(jnp.where(child < cut, in_a, in_b))
+                for number, x in enumerate(panels):
+                    high, low = split(x)
+                    at = pl.ds(pl.multiple_of((here ^ number) * part, part), part)
+                    panel_ref[at, :] = jnp.concatenate([high, low], axis=1)
+                full = dense_columns(held[group["col_map"]][child], panel_ref, cols)
+                depth = full.shape[1] // 2
+                full_high, full_low = full[:, :depth], full[:, depth:]
+                dense_high, dense_low = full_high.astype(BF16), full_low.astype(BF16)
+                staged[0][child] = dense_high
+                staged[1][child] = dense_low
+                for n in range(2):
+                    dense_copy(n, child).start()
+
+                for c in range(plan["sums"]):
+
+                    @pl.when(child == c)
+                    def _(c=c):
+                        staged[2 + c][0] = full_high + full_low
+                        dense_copy(2 + c, 0).start()
+
+            else:
+                for i in group["dense"]:
+                    one(i, child).wait()
+                if len(group["dense"]) == 2:
+                    dense_high, dense_low = (held[i][child] for i in group["dense"])
+                else:
+                    dense_high, dense_low = split(held[group["dense"][0]][child])
+            panels = []
+            for place, first, which, members in group["chunks"]:
+                panels.append(sum(held[m][child] for m in members))
+                at = pl.ds(pl.multiple_of((child + offset(first)) * part, part), part)
+                slots_ref[place, :, at] = held[group["map"]][child, pl.ds(ids[which], 1), :]
+            high, low = split(jnp.concatenate(panels, axis=0))
+            both = dot_t(jnp.concatenate([high, low], axis=0), dense_high)
+            count = high.shape[0]
+            n_high, n_low = split(both[:count] + both[count:] + dot_t(high, dense_low))
+            for number, (place, first, _, _) in enumerate(group["chunks"]):
+                cut = slice(number * part, (number + 1) * part)
+                at = pl.ds(pl.multiple_of((child + offset(first)) * part, part), part)
+                high_ref[place, at, :] = n_high[cut]
+                low_ref[place, at, :] = n_low[cut]
+            return carry
+
+        lax.fori_loop(0, group["count"], narrow, 0)
+
+    def finish(block, carry):
+        at = pl.ds(pl.multiple_of(block * rows, rows), rows)
+        if bases:
+            for n in range(len(bases)):
+                base_copy(n, block).wait()
+            if plan["one_layer"]:
+                acc[at, :] = jnp.where(layer == 0, acc[at, :], 0.0)
+            if len(bases) > 1:
+                acc[at, :] += sum(e[at, :] for e in extra)
+        else:
+            acc[at, :] = jnp.zeros((rows, cols), F32)
+        for place, (which, count) in enumerate(plan["places"]):
+            used = count * part
+
+            @pl.when(ids[which] <= block)
+            def _(place=place, used=used):
+                hot = one_hot(slots_ref[place, :, :used], block * rows, rows)
+                acc[at, :] -= dot(hot, high_ref[place, :used]) + dot(hot, low_ref[place, :used])
+
+        for piece in range(plan["pieces"]):
+
+            @pl.when((block >= piece * each) & (block < (piece + 1) * each))
+            def _(piece=piece):
+                out_copy(block, piece).start()
+
+        return carry
+
+    lax.fori_loop(0, blocks, finish, 0)
+    for block in range(blocks):
+        out_copy(block, block // each).wait()
+    for n in range(n_staged):
+        for child in range(plan["groups"][0]["count"] if n < 2 else 1):
+            dense_copy(n, child).wait()
+
+
+def stage(shape, bases, places, groups, emit_sums=None, pieces=1, one_layer=False):
+    row_count, col_count = shape
+    inputs, base_at = [], []
+    for base in bases:
+        base_at.append(list(range(len(inputs), len(inputs) + len(base))))
+        inputs += base
+    held, ranges, single, layout = [], {}, [], []
+
+    def take(pair, count):
+        array, first = pair
+        low, high = max(first, 0), min(first + count, array.shape[0])
+        if high <= low:
+            low, high = 0, 1
+        inputs.append(array)
+        held.append(len(inputs) - 1)
+        ranges[held[-1]] = (low, high - low)
+        return held[-1]
+
+    for g in groups:
+        count = g["count"]
+        item = dict(count=count, map=take(g["map"], count), dense=[])
+        if "u" in g:
+            item["col_map"] = take(g["col_map"], count)
+            item["u"] = [take(p, count) for p in g["u"]]
+            item["cut"] = g["cut"]
+        else:
+            item["dense"] = [take(p, count) for p in g["dense"]]
+            single += item["dense"]
+        item["chunks"] = [
+            (place, first, places[place][0], [take(p, count) for p in panels])
+            for place, first, panels in g["chunks"]
+        ]
+        part, depth = g["chunks"][0][2][0][0].shape[1:]
+        layout.append(item)
+    rows = 2 * part
+    most = max(count for _, count in places)
+    total = groups[0]["count"]
+    out_shape = [jax.ShapeDtypeStruct((row_count // pieces, col_count), F32)] * pieces
+    emit = emit_sums is not None
+    sums = emit_sums or 0
+    dense_shapes = [((total, col_count, depth), BF16)] * (2 * emit) + [((1, col_count, depth), F32)] * sums
+    out_shape += [jax.ShapeDtypeStruct(*x) for x in dense_shapes]
+    plan = dict(
+        inputs=len(inputs),
+        outputs=len(out_shape),
+        bases=base_at,
+        pieces=pieces,
+        held=held,
+        range=ranges,
+        single=single,
+        groups=layout,
+        places=places,
+        emit=emit,
+        sums=sums,
+        one_layer=one_layer,
+        part=part,
+        rows=rows,
+    )
+    deepest = max(g["count"] for g in groups)
+    blocks = row_count // rows
+    kept = set(single)
+    buffers = (
+        [((ranges[i][1],) + inputs[i].shape[1:], inputs[i].dtype) for i in held]
+        + [
+            (shape, F32),
+            ((len(places), 1, most * part), jnp.int32),
+            ((len(places), most * part, col_count), BF16),
+            ((len(places), most * part, col_count), BF16),
+        ]
+        + dense_shapes
+        + [(shape, F32)] * max(len(bases) - 1, 0)
+        + [((4 * part, 2 * depth), BF16)]
+    )
+    return pl.pallas_call(
+        functools.partial(stage_kernel, plan),
+        in_specs=[pl.BlockSpec(memory_space=pl.ANY if i in kept else pltpu.HBM) for i in range(len(inputs))],
+        out_specs=[pl.BlockSpec(memory_space=pltpu.HBM)] * pieces + [pl.BlockSpec(memory_space=pl.ANY)] * len(dense_shapes),
+        out_shape=out_shape,
+        scratch_shapes=[pltpu.VMEM(dims, kind) for dims, kind in buffers]
+        + [
+            pltpu.SemaphoreType.DMA((len(held), deepest)),
+            pltpu.SemaphoreType.DMA((max(len(bases), 1), blocks)),
+            pltpu.SemaphoreType.DMA((1 + len(dense_shapes), max(blocks, total))),
+        ],
+        compiler_params=pltpu.CompilerParams(vmem_limit_bytes=VMEM_ALL),
+        cost_estimate=pl.CostEstimate(flops=1000, bytes_accessed=1000, transcendentals=0),
+    )(*inputs)
+
+
+ENDS = [(0, 1), (1, 0), (2, 3), (3, 2)]
+MIDDLE = [(1, 2), (2, 1)]
+OUTWARD = [(1, 0), (2, 3)]
+SWAP_X = [(0, 1), (1, 0), (2, 3), (3, 2)]
+SWAP_Y = [(0, 2), (2, 0), (1, 3), (3, 1)]
+SWAP_XY = [(0, 3), (3, 0), (1, 2), (2, 1)]
+
+
+def four_by_four(front_matrix, l_panels, l_map, u_panels, u_map):
+    shape = front_matrix.shape
+    l_own = l_panels[0, :, 0]
+    u_own = u_panels[0, :, 0]
+    children = u_own.shape[0]
+    first = children // 2
+    late = children * 3 // 8
+    rest, early = children - first, children - late
+    row_map = l_map.reshape(children, 4, -1)
+    col_map = u_map.reshape(children, 1, -1)
+    swap = [(0, 1), (1, 0)]
+    together = lax.optimization_barrier
+
+    quarter = first // 2
+    pair = lax.ppermute(l_own, "col", ENDS)
+    mid_b = lax.ppermute(l_own, "col", MIDDLE)
+    by_x = lax.ppermute(u_own, "row", SWAP_X)
+    by_y = lax.ppermute(u_own, "row", SWAP_Y)
+    pair, mid_b, by_x, by_y = together((pair, mid_b, by_x, by_y))
+
+    def diagonal(start):
+        cut = start + quarter
+        return (
+            lax.ppermute(by_x[start:cut], "row", SWAP_Y),
+            lax.ppermute(by_y[cut : start + first], "row", SWAP_X),
+        )
+
+    by_xy1 = diagonal(0)
+    far_b = lax.ppermute(pair, "col", MIDDLE)
+    mid_a = lax.ppermute(mid_b, "col", OUTWARD)
+    by_xy2 = diagonal(first)
+    row_map_other = lax.ppermute(row_map, "gz", swap)
+
+    def near(base, start, u, chunks=(), groups=(), **options):
+        group = dict(
+            count=first,
+            map=(row_map, start),
+            col_map=(col_map, start),
+            u=[(u_own, start), (by_x, start), (by_y, start)] + [(x, 0) for x in u],
+            cut=quarter,
+            chunks=[(0, 0, [(l_own, start)]), (1, 0, [(pair, start)]), *chunks],
+        )
+        places = [(0, first), (1, first)] + [(2, children)] * len(chunks)
+        return stage(shape, [base], places, [group, *groups], **options)
+
+    mine, *dense1 = near([front_matrix], 0, by_xy1, emit_sums=late, one_layer=True)
+    dense1, sums = dense1[:2], dense1[2:]
+    far_b, mine = together((far_b, mine))
+    far_b2, far_b1 = far_b[:late], far_b[late:]
+    far_a1 = lax.ppermute(far_b1, "col", OUTWARD)
+    far_a2 = lax.ppermute(far_b2, "col", OUTWARD)
+    far_b2_other = lax.ppermute(far_b2, "gz", swap)
+    *sums, by_xy2a, by_xy2b = together((*sums, *by_xy2))
+    sums_other = [lax.ppermute(x, "gz", swap) for x in sums]
+    mine, *dense2 = near(
+        [mine],
+        first,
+        (by_xy2a, by_xy2b),
+        [(2, first, [(mid_a, first), (mid_b, first)])],
+        [
+            dict(
+                count=first,
+                map=(row_map, 0),
+                dense=[(d, 0) for d in dense1],
+                chunks=[(2, 0, [(mid_a, 0), (mid_b, 0)])],
+            )
+        ],
+        emit_sums=0,
+    )
+    mine, far_b2_other, *sums_other = together((mine, far_b2_other, *sums_other))
+    top, bottom = stage(
+        shape,
+        [[mine]],
+        [(3, early)],
+        [
+            dict(
+                count=first - late,
+                map=(row_map, late),
+                dense=[(d, late) for d in dense1],
+                chunks=[(0, 0, [(far_a1, 0), (far_b1, 0)])],
+            ),
+            dict(
+                count=rest,
+                map=(row_map, first),
+                dense=[(d, 0) for d in dense2],
+                chunks=[(0, first - late, [(far_a1, first - late), (far_b1, first - late)])],
+            ),
+        ],
+        pieces=2,
+    )
+    other_top = lax.ppermute(top, "gz", swap)
+    sent, far_a2 = together((bottom, far_a2))
+    far_a2_other = lax.ppermute(far_a2, "gz", swap)
+    other_bottom = lax.ppermute(sent, "gz", swap)
+    late_groups = [
+        dict(
+            count=1,
+            map=(slot_map, c),
+            dense=[(x, 0)],
+            chunks=[(0, at, [(far, c) for far in fars])],
+        )
+        for slot_map, denses, fars, at in (
+            (row_map, sums, (far_a2, far_b2), lambda layer: layer * late),
+            (row_map_other, sums_other, (far_a2_other, far_b2_other), lambda layer: (1 - layer) * late),
+        )
+        for c, x in enumerate(denses)
+    ]
+    for g in late_groups:
+        place, at, fars = g["chunks"][0]
+        g["chunks"] = [(place, functools.partial(lambda at, c, layer: at(layer) + c, at, g["map"][1]), fars)]
+    (out,) = stage(shape, [[top, bottom], [other_top, other_bottom]], [(3, 2 * late)], late_groups)
+    return out
+
+
 def solution(mesh):
     placed = (
         P("row", "col"),
@@ -33,6 +437,11 @@
         P("gz", None, "col", "row", None),
         P("gz", None, "col", None),
     )
+    square = mesh.shape["row"] == 4 and mesh.shape["col"] == 4
     return jax.shard_map(
-        shards, mesh=mesh, in_specs=placed, out_specs=P("row", "col"), check_vma=False
-    )
+        four_by_four if square else any_mesh,
+        mesh=mesh,
+        in_specs=placed,
+        out_specs=P("row", "col"),
+        check_vma=False,
+    )

time: 235 us -> 114 us (0.49)
  the two profiles are of different devices: /device:TPU:0 before, /device:TPU:19 now
where the time goes in v2:
time: 114 us; the launch traced here: 113 us
  Pallas kernels  51.6 us (45%)
  waiting for transfers between devices  30.2 us (26%)
  starting transfers between devices  26.6 us (23%)
  local copies, waits for them, and re-layouts  4.55 us (4%)
    pallas_call x4, Pallas kernels, stage(): pl.pallas_call(functools.partial(stage_kernel, plan), in_specs=[pl.BlockS...  51.6 us
    ppermute x1, waiting for transfers between devices, four_by_four(): pair = lax.ppermute(l_own, 'col', ENDS)  19.6 us
    ppermute x1, waiting for transfers between devices, four_by_four(): row_map_other = lax.ppermute(row_map, 'gz', swap)  5.07 us
    ppermute x3, starting transfers between devices, four_by_four(): sums_other = [lax.ppermute(x, 'gz', swap) for x in sums]  3.98 us
    ppermute x1, starting transfers between devices, four_by_four(): far_b2_other = lax.ppermute(far_b2, 'gz', swap)  3.29 us
    ppermute x1, starting transfers between devices, four_by_four(): far_a2 = lax.ppermute(far_b2, 'col', OUTWARD)  3.12 us
    ppermute x1, starting transfers between devices, four_by_four(): far_b = lax.ppermute(pair, 'col', MIDDLE)  2.97 us
    ppermute x1, waiting for transfers between devices, four_by_four(): mid_b = lax.ppermute(l_own, 'col', MIDDLE)  2.86 us
  transfers between devices with their start and end apart: 20, of which 6 were waited for; matrix products, arithmetic and copies ran while one was open for 3% of the time, Pallas kernels for 35%

profile of v2, /device:TPU:19, one launch (start us, length us, event | category | flops | bytes accessed | tf_op | source)
XLA Modules:
  0.0 113.3 jit_solution(2440255302032335395)
XLA Ops:
  0.0 1.3 %collective-permute-start = (f32[8,128,256]{2,1,0:T(8,128)}, f32[8,128,256]{2,1,0:T(8,128)S(1)}, u32[]{:S(2)}, u32[]{:S(2)}) collective-permute-start(f32[8,128,256]{2,1,0:T(8,128)} %bitcast.8), channel_id=1, source_target_pairs={{0,1},{1,0},{2,3},{3,2},{4,5},{5,4},{6,7},{7,6},{8,9},{9,8},{10,11... | collective-permute-start | bytes 3145736 | tf_op jit(solution)/shard_map/ppermute | solution.py:332
  1.3 1.9 %collective-permute-start.1 = (f32[8,128,256]{2,1,0:T(8,128)}, f32[8,128,256]{2,1,0:T(8,128)}, u32[]{:S(2)}, u32[]{:S(2)}) collective-permute-start(f32[8,128,256]{2,1,0:T(8,128)} %bitcast.9), channel_id=1, source_target_pairs={{1,2},{2,1},{5,6},{6,5},{9,10},{10,9},{13,14},{14,13},{17,18},{18,... | collective-permute-start | bytes 3145736 | tf_op jit(solution)/shard_map/ppermute | solution.py:333
  3.2 0.3 collective-permute-start.2
  3.5 1.2 %collective-permute-start.3 = (f32[8,128,256]{2,1,0:T(8,128)}, f32[8,128,256]{2,1,0:T(8,128)S(1)}, u32[]{:S(2)}, u32[]{:S(2)}) collective-permute-start(f32[8,128,256]{2,1,0:T(8,128)} %bitcast.5), channel_id=1, source_target_pairs={{0,8},{8,0},{4,12},{12,4},{1,9},{9,1},{5,13},{13,5},{2,10},{10,2},... | collective-permute-start | bytes 3145736 | tf_op jit(solution)/shard_map/ppermute | solution.py:335
  4.8 19.6 %collective-permute-done.refs_9_ = f32[8,128,256]{2,1,0:T(8,128)S(1)} collective-permute-done((f32[8,128,256]{2,1,0:T(8,128)}, f32[8,128,256]{2,1,0:T(8,128)S(1)}, u32[]{:S(2)}, u32[]{:S(2)}) %collective-permute-start) | collective-permute-done | bytes 1048608 | tf_op jit(solution)/shard_map/ppermute | solution.py:332
  24.3 2.9 %collective-permute-done.1.refs_11_.refs_16_ = f32[8,128,256]{2,1,0:T(8,128)} collective-permute-done((f32[8,128,256]{2,1,0:T(8,128)}, f32[8,128,256]{2,1,0:T(8,128)}, u32[]{:S(2)}, u32[]{:S(2)}) %collective-permute-start.1) | collective-permute-done | bytes 1048608 | tf_op jit(solution)/shard_map/ppermute | solution.py:333
  27.4 1.3 %collective-permute-start.5 = (f32[2,128,256]{2,1,0:T(8,128)S(1)}, f32[2,128,256]{2,1,0:T(8,128)S(1)}, u32[]{:S(2)}, u32[]{:S(2)}) collective-permute-start(f32[2,128,256]{2,1,0:T(8,128)S(1)} %get-tuple-element.66), channel_id=1, source_target_pairs={{0,8},{8,0},{4,12},{12,4},{1,9},{9,1},{5,13},{13,5},{2,10},{10,2},... | collective-permute-start | bytes 786440 | tf_op jit(solution)/shard_map/ppermute | solution.py:341
  28.7 0.7 fusion
  29.4 1.2 %collective-permute-start.6 = (f32[2,128,256]{2,1,0:T(8,128)S(1)}, f32[2,128,256]{2,1,0:T(8,128)S(1)}, u32[]{:S(2)}, u32[]{:S(2)}) collective-permute-start(f32[2,128,256]{2,1,0:T(8,128)S(1)} %get-tuple-element.64), channel_id=1, source_target_pairs={{0,4},{4,0},{8,12},{12,8},{1,5},{5,1},{9,13},{13,9},{2,6},{6,2},{1... | collective-permute-start | bytes 786440 | tf_op jit(solution)/shard_map/ppermute | solution.py:342
  30.6 3.0 %collective-permute-start.4 = (f32[8,128,256]{2,1,0:T(8,128)S(1)}, f32[8,128,256]{2,1,0:T(8,128)}, u32[]{:S(2)}, u32[]{:S(2)}) collective-permute-start(f32[8,128,256]{2,1,0:T(8,128)S(1)} %collective-permute-done.refs_9_), channel_id=1, source_target_pairs={{1,2},{2,1},{5,6},{6,5},{9,10},{10,9},{13,14},{14,13},{17,18},{18,... | collective-permute-start | bytes 3145736 | tf_op jit(solution)/shard_map/ppermute | solution.py:346
  33.5 0.3 collective-permute-start.7
  33.8 0.7 collective-permute-start.8
  34.5 2.3 %collective-permute-start.9 = (f32[8,128,256]{2,1,0:T(8,128)}, f32[8,128,256]{2,1,0:T(8,128)}, u32[]{:S(2)}, u32[]{:S(2)}) collective-permute-start(f32[8,128,256]{2,1,0:T(8,128)} %collective-permute-done.1.refs_11_.refs_16_), channel_id=1, source_target_pairs={{1,0},{2,3},{5,4},{6,7},{9,8},{10,11},{13,12},{14,15},{17,16},{18,... | collective-permute-start | bytes 3145736 | tf_op jit(solution)/shard_map/ppermute | solution.py:347
  36.8 0.7 copy-done.13
  37.5 12.5 %shard_map.55 = (f32[1024,1024]{1,0:T(8,128)}, bf16[4,1024,256]{2,1,0:T(8,128)(2,1)}, bf16[4,1024,256]{2,1,0:T(8,128)(2,1)}, f32[1,1024,256]{2,1,0:T(8,128)}, f3...) custom-call(f32[1024,1024]{1,0:T(8,128)} %refs_0_.1, s32[8,4,128]{2,1,0:T(4,128)} %bitcast.12, s32[8,1,512]{2,1,0:T(1,128)} %bitcast.21, ...), custom_call_target="tpu_custom_call" | custom-call | flops 1000 | bytes 1000 | tf_op jit(solution)/shard_map/pallas_call | solution.py:294
  50.0 3.5 %collective-permute-start.11 = (f32[1,1024,256]{2,1,0:T(8,128)}, f32[1,1024,256]{2,1,0:T(8,128)S(1)}, u32[]{:S(2)}, u32[]{:S(2)}) collective-permute-start(f32[1,1024,256]{2,1,0:T(8,128)} %get-tuple-element.49.refs_5_), channel_id=1, source_target_pairs={{0,16},{16,0},{1,17},{17,1},{2,18},{18,2},{3,19},{19,3},{4,20},{20... | collective-permute-start | bytes 3145736 | tf_op jit(solution)/shard_map/ppermute | solution.py:371
  53.6 0.4 collective-permute-start.13
  54.0 0.6 collective-permute-done.4
  54.6 1.1 %slice.23.refs_5_.refs_10_ = f32[5,128,256]{2,1,0:T(8,128)S(1)} slice(f32[8,128,256]{2,1,0:T(8,128)} %collective-permute-done.4), slice={[3:8], [0:128], [0:256]} | slice | bytes 1310720 | tf_op jit(solution)/shard_map/slice | solution.py:366
  55.7 1.6 %collective-permute-start.14 = (f32[5,128,256]{2,1,0:T(8,128)S(1)}, f32[5,128,256]{2,1,0:T(8,128)S(1)}, u32[]{:S(2)}, u32[]{:S(2)}) collective-permute-start(f32[5,128,256]{2,1,0:T(8,128)S(1)} %slice.23.refs_5_.refs_10_), channel_id=1, source_target_pairs={{1,0},{2,3},{5,4},{6,7},{9,8},{10,11},{13,12},{14,15},{17,16},{18,... | collective-permute-start | bytes 1966088 | tf_op jit(solution)/shard_map/ppermute | solution.py:367
  57.4 1.0 slice.22.refs_7_.refs_11_.refs_15_
  58.4 3.3 %collective-permute-start.10 = (f32[3,128,256]{2,1,0:T(8,128)S(1)}, f32[3,128,256]{2,1,0:T(8,128)S(1)}, u32[]{:S(2)}, u32[]{:S(2)}) collective-permute-start(f32[3,128,256]{2,1,0:T(8,128)S(1)} %slice.22.refs_7_.refs_11_.refs_15_), channel_id=1, source_target_pairs={{0,16},{16,0},{1,17},{17,1},{2,18},{18,2},{3,19},{19,3},{4,20},{20... | collective-permute-start | bytes 1179656 | tf_op jit(solution)/shard_map/ppermute | solution.py:369
  61.7 3.1 %collective-permute-start.16 = (f32[3,128,256]{2,1,0:T(8,128)S(1)}, f32[3,128,256]{2,1,0:T(8,128)S(1)}, u32[]{:S(2)}, u32[]{:S(2)}) collective-permute-start(f32[3,128,256]{2,1,0:T(8,128)S(1)} %slice.22.refs_7_.refs_11_.refs_15_), channel_id=1, source_target_pairs={{1,0},{2,3},{5,4},{6,7},{9,8},{10,11},{13,12},{14,15},{17,16},{18,... | collective-permute-start | bytes 1179656 | tf_op jit(solution)/shard_map/ppermute | solution.py:368
  64.9 17.2 %shard_map.56 = (f32[1024,1024]{1,0:T(8,128)}, bf16[4,1024,256]{2,1,0:T(8,128)(2,1)}, bf16[4,1024,256]{2,1,0:T(8,128)(2,1)}) custom-call(f32[1024,1024]{1,0:T(8,128)} %get-tuple-element.38.refs_0_, s32[8,4,128]{2,1,0:T(4,128)} %bitcast.13, s32[8,1,512]{2,1,0:T(1,128)} %bitcast.22, f32[8,128,256]{2,1,0:T(8,128)} %bitcast.7, f32[8,128,256]{2,1,0:T(8,128)} %copy-done, ...), custom_call_target="tpu_custom_call" | custom-call | flops 1000 | bytes 1000 | tf_op jit(solution)/shard_map/pallas_call | solution.py:294
  82.2 0.9 copy-done.8
  83.0 9.7 %shard_map.57 = (f32[512,1024]{1,0:T(8,128)}, f32[512,1024]{1,0:T(8,128)}) custom-call(f32[1024,1024]{1,0:T(8,128)} %get-tuple-element.52.refs_0_, s32[8,4,128]{2,1,0:T(4,128)} %bitcast.15, bf16[4,1024,256]{2,1,0:T(8,128)(2,1)} %get-tuple-element.45.refs_13_.refs_2_, bf16[4,1024,256]{2,1,0:T(8,128)(2,1)} %get-tuple-element.46.refs_14_.refs_3_, ...), custom_call_target="tpu_custom_call" | custom-call | flops 1000 | bytes 1000 | tf_op jit(solution)/shard_map/pallas_call | solution.py:294
  92.8 0.4 collective-permute-start.17
  93.1 0.2 collective-permute-start.15
  93.4 0.3 collective-permute-start.19
  93.9 5.1 %collective-permute-done.18.refs_16_.refs_20_.refs_24_ = s32[8,4,128]{2,1,0:T(4,128)S(1)} collective-permute-done((s32[8,4,128]{2,1,0:T(4,128)S(1)}, s32[8,4,128]{2,1,0:T(4,128)S(1)}, u32[]{:S(2)}, u32[]{:S(2)}) %collective-permute-start.18) | collective-permute-done | bytes 16416 | tf_op jit(solution)/shard_map/ppermute | solution.py:349
  99.0 2.0 %collective-permute-done.15.refs_2_ = f32[512,1024]{1,0:T(8,128)} collective-permute-done((f32[512,1024]{1,0:T(8,128)}, f32[512,1024]{1,0:T(8,128)}, u32[]{:S(2)}, u32[]{:S(2)}) %collective-permute-start.15) | collective-permute-done | bytes 2097184 | tf_op jit(solution)/shard_map/ppermute | solution.py:408
  101.0 12.1 %shard_map.58 = f32[1024,1024]{1,0:T(8,128)} custom-call(f32[512,1024]{1,0:T(8,128)} %get-tuple-element.55.refs_0_, f32[512,1024]{1,0:T(8,128)} %get-tuple-element.57.refs_1_, f32[512,1024]{1,0:T(8,128)} %collective-permute-done.15.refs_2_, f32[512,1024]{1,0:T(8,128)} %copy-done.9, s32[8,4,128]{2,1,0:T(4,128)} %bitcast.17, ...), custom_call_target="tpu_custom_call" | custom-call | flops 1000 | bytes 1000 | tf_op jit(solution)/shard_map/pallas_call | solution.py:294
  (46 shorter events, 0.5 us)
Async XLA Ops:
  0.0 24.3 %collective-permute-start = (f32[8,128,256]{2,1,0:T(8,128)}, f32[8,128,256]{2,1,0:T(8,128)S(1)}, u32[]{:S(2)}, u32[]{:S(2)}) collective-permute-start(f32[8,128,256]{2,1,0:T(8,128)} %bitcast.8), channel_id=1, source_target_pairs={{0,1},{1,0},{2,3},{3,2},{4,5},{5,4},{6,7},{7,6},{8,9},{9,8},{10,11... | collective-permute-start | bytes 3145736 | tf_op jit(solution)/shard_map/ppermute | solution.py:332
  1.3 25.9 %collective-permute-start.1 = (f32[8,128,256]{2,1,0:T(8,128)}, f32[8,128,256]{2,1,0:T(8,128)}, u32[]{:S(2)}, u32[]{:S(2)}) collective-permute-start(f32[8,128,256]{2,1,0:T(8,128)} %bitcast.9), channel_id=1, source_target_pairs={{1,2},{2,1},{5,6},{6,5},{9,10},{10,9},{13,14},{14,13},{17,18},{18,... | collective-permute-start | bytes 3145736 | tf_op jit(solution)/shard_map/ppermute | solution.py:333
  3.2 24.1 %collective-permute-start.2 = (f32[8,128,256]{2,1,0:T(8,128)}, f32[8,128,256]{2,1,0:T(8,128)S(1)}, u32[]{:S(2)}, u32[]{:S(2)}) collective-permute-start(f32[8,128,256]{2,1,0:T(8,128)} %bitcast.4), channel_id=1, source_target_pairs={{0,4},{4,0},{8,12},{12,8},{1,5},{5,1},{9,13},{13,9},{2,6},{6,2},{1... | collective-permute-start | bytes 3145736 | tf_op jit(solution)/shard_map/ppermute | solution.py:334
  3.5 23.8 %collective-permute-start.3 = (f32[8,128,256]{2,1,0:T(8,128)}, f32[8,128,256]{2,1,0:T(8,128)S(1)}, u32[]{:S(2)}, u32[]{:S(2)}) collective-permute-start(f32[8,128,256]{2,1,0:T(8,128)} %bitcast.5), channel_id=1, source_target_pairs={{0,8},{8,0},{4,12},{12,4},{1,9},{9,1},{5,13},{13,5},{2,10},{10,2},... | collective-permute-start | bytes 3145736 | tf_op jit(solution)/shard_map/ppermute | solution.py:335
  24.3 12.4 %copy-start.4 = (f32[8,128,256]{2,1,0:T(8,128)}, f32[8,128,256]{2,1,0:T(8,128)S(1)}, u32[]{:S(2)}) copy-start(f32[8,128,256]{2,1,0:T(8,128)S(1)} %collective-permute-done.refs_9_) | copy-start | bytes 3145732
  27.3 9.5 %copy-start = (f32[8,128,256]{2,1,0:T(8,128)}, f32[8,128,256]{2,1,0:T(8,128)S(1)}, u32[]{:S(2)}) copy-start(f32[8,128,256]{2,1,0:T(8,128)S(1)} %collective-permute-done.2.refs_4_) | copy-start | bytes 3145732
  27.3 9.5 %copy-start.1 = (f32[8,128,256]{2,1,0:T(8,128)}, f32[8,128,256]{2,1,0:T(8,128)S(1)}, u32[]{:S(2)}) copy-start(f32[8,128,256]{2,1,0:T(8,128)S(1)} %collective-permute-done.3.refs_5_) | copy-start | bytes 3145732
  27.4 7.2 %collective-permute-start.5 = (f32[2,128,256]{2,1,0:T(8,128)S(1)}, f32[2,128,256]{2,1,0:T(8,128)S(1)}, u32[]{:S(2)}, u32[]{:S(2)}) collective-permute-start(f32[2,128,256]{2,1,0:T(8,128)S(1)} %get-tuple-element.66), channel_id=1, source_target_pairs={{0,8},{8,0},{4,12},{12,4},{1,9},{9,1},{5,13},{13,5},{2,10},{10,2},... | collective-permute-start | bytes 786440 | tf_op jit(solution)/shard_map/ppermute | solution.py:341
  29.4 7.4 %collective-permute-start.6 = (f32[2,128,256]{2,1,0:T(8,128)S(1)}, f32[2,128,256]{2,1,0:T(8,128)S(1)}, u32[]{:S(2)}, u32[]{:S(2)}) collective-permute-start(f32[2,128,256]{2,1,0:T(8,128)S(1)} %get-tuple-element.64), channel_id=1, source_target_pairs={{0,4},{4,0},{8,12},{12,8},{1,5},{5,1},{9,13},{13,9},{2,6},{6,2},{1... | collective-permute-start | bytes 786440 | tf_op jit(solution)/shard_map/ppermute | solution.py:342
  30.6 24.0 %collective-permute-start.4 = (f32[8,128,256]{2,1,0:T(8,128)S(1)}, f32[8,128,256]{2,1,0:T(8,128)}, u32[]{:S(2)}, u32[]{:S(2)}) collective-permute-start(f32[8,128,256]{2,1,0:T(8,128)S(1)} %collective-permute-done.refs_9_), channel_id=1, source_target_pairs={{1,2},{2,1},{5,6},{6,5},{9,10},{10,9},{13,14},{14,13},{17,18},{18,... | collective-permute-start | bytes 3145736 | tf_op jit(solution)/shard_map/ppermute | solution.py:346
  33.5 16.5 %collective-permute-start.7 = (f32[2,128,256]{2,1,0:T(8,128)S(1)}, f32[2,128,256]{2,1,0:T(8,128)}, u32[]{:S(2)}, u32[]{:S(2)}) collective-permute-start(f32[2,128,256]{2,1,0:T(8,128)S(1)} %get-tuple-element.65), channel_id=1, source_target_pairs={{0,8},{8,0},{4,12},{12,4},{1,9},{9,1},{5,13},{13,5},{2,10},{10,2},... | collective-permute-start | bytes 786440 | tf_op jit(solution)/shard_map/ppermute | solution.py:341
  33.8 16.2 %collective-permute-start.8 = (f32[2,128,256]{2,1,0:T(8,128)}, f32[2,128,256]{2,1,0:T(8,128)}, u32[]{:S(2)}, u32[]{:S(2)}) collective-permute-start(f32[2,128,256]{2,1,0:T(8,128)} %get-tuple-element.63), channel_id=1, source_target_pairs={{0,4},{4,0},{8,12},{12,8},{1,5},{5,1},{9,13},{13,9},{2,6},{6,2},{1... | collective-permute-start | bytes 786440 | tf_op jit(solution)/shard_map/ppermute | solution.py:342
  34.5 2.3 %copy-start.12 = (f32[2,128,256]{2,1,0:T(8,128)}, f32[2,128,256]{2,1,0:T(8,128)S(1)}, u32[]{:S(2)}) copy-start(f32[2,128,256]{2,1,0:T(8,128)S(1)} %collective-permute-done.5.refs_6_) | copy-start | bytes 786436
  34.5 23.9 %collective-permute-start.9 = (f32[8,128,256]{2,1,0:T(8,128)}, f32[8,128,256]{2,1,0:T(8,128)}, u32[]{:S(2)}, u32[]{:S(2)}) collective-permute-start(f32[8,128,256]{2,1,0:T(8,128)} %collective-permute-done.1.refs_11_.refs_16_), channel_id=1, source_target_pairs={{1,0},{2,3},{5,4},{6,7},{9,8},{10,11},{13,12},{14,15},{17,16},{18,... | collective-permute-start | bytes 3145736 | tf_op jit(solution)/shard_map/ppermute | solution.py:347
  50.0 11.7 %collective-permute-start.11 = (f32[1,1024,256]{2,1,0:T(8,128)}, f32[1,1024,256]{2,1,0:T(8,128)S(1)}, u32[]{:S(2)}, u32[]{:S(2)}) collective-permute-start(f32[1,1024,256]{2,1,0:T(8,128)} %get-tuple-element.49.refs_5_), channel_id=1, source_target_pairs={{0,16},{16,0},{1,17},{17,1},{2,18},{18,2},{3,19},{19,3},{4,20},{20... | collective-permute-start | bytes 3145736 | tf_op jit(solution)/shard_map/ppermute | solution.py:371
  53.5 28.6 %collective-permute-start.12 = (f32[1,1024,256]{2,1,0:T(8,128)}, f32[1,1024,256]{2,1,0:T(8,128)}, u32[]{:S(2)}, u32[]{:S(2)}) collective-permute-start(f32[1,1024,256]{2,1,0:T(8,128)} %get-tuple-element.50.refs_9_), channel_id=1, source_target_pairs={{0,16},{16,0},{1,17},{17,1},{2,18},{18,2},{3,19},{19,3},{4,20},{20... | collective-permute-start | bytes 3145736 | tf_op jit(solution)/shard_map/ppermute | solution.py:371
  53.6 28.5 %collective-permute-start.13 = (f32[1,1024,256]{2,1,0:T(8,128)}, f32[1,1024,256]{2,1,0:T(8,128)}, u32[]{:S(2)}, u32[]{:S(2)}) collective-permute-start(f32[1,1024,256]{2,1,0:T(8,128)} %get-tuple-element.51.refs_13_), channel_id=1, source_target_pairs={{0,16},{16,0},{1,17},{17,1},{2,18},{18,2},{3,19},{19,3},{4,20},{20... | collective-permute-start | bytes 3145736 | tf_op jit(solution)/shard_map/ppermute | solution.py:371
  55.7 26.4 %copy-start.3 = (f32[5,128,256]{2,1,0:T(8,128)}, f32[5,128,256]{2,1,0:T(8,128)S(1)}, u32[]{:S(2)}) copy-start(f32[5,128,256]{2,1,0:T(8,128)S(1)} %slice.23.refs_5_.refs_10_) | copy-start | bytes 1966084
  55.7 26.4 %collective-permute-start.14 = (f32[5,128,256]{2,1,0:T(8,128)S(1)}, f32[5,128,256]{2,1,0:T(8,128)S(1)}, u32[]{:S(2)}, u32[]{:S(2)}) collective-permute-start(f32[5,128,256]{2,1,0:T(8,128)S(1)} %slice.23.refs_5_.refs_10_), channel_id=1, source_target_pairs={{1,0},{2,3},{5,4},{6,7},{9,8},{10,11},{13,12},{14,15},{17,16},{18,... | collective-permute-start | bytes 1966088 | tf_op jit(solution)/shard_map/ppermute | solution.py:367
  58.4 23.7 %copy-start.2 = (f32[3,128,256]{2,1,0:T(8,128)}, f32[3,128,256]{2,1,0:T(8,128)S(1)}, u32[]{:S(2)}) copy-start(f32[3,128,256]{2,1,0:T(8,128)S(1)} %slice.22.refs_7_.refs_11_.refs_15_) | copy-start | bytes 1179652
  58.4 23.7 %collective-permute-start.10 = (f32[3,128,256]{2,1,0:T(8,128)S(1)}, f32[3,128,256]{2,1,0:T(8,128)S(1)}, u32[]{:S(2)}, u32[]{:S(2)}) collective-permute-start(f32[3,128,256]{2,1,0:T(8,128)S(1)} %slice.22.refs_7_.refs_11_.refs_15_), channel_id=1, source_target_pairs={{0,16},{16,0},{1,17},{17,1},{2,18},{18,2},{3,19},{19,3},{4,20},{20... | collective-permute-start | bytes 1179656 | tf_op jit(solution)/shard_map/ppermute | solution.py:369
  61.7 20.4 %copy-start.10 = (f32[1,1024,256]{2,1,0:T(8,128)}, f32[1,1024,256]{2,1,0:T(8,128)S(1)}, u32[]{:S(2)}) copy-start(f32[1,1024,256]{2,1,0:T(8,128)S(1)} %collective-permute-done.11.refs_17_) | copy-start | bytes 3145732
  61.7 31.0 %collective-permute-start.16 = (f32[3,128,256]{2,1,0:T(8,128)S(1)}, f32[3,128,256]{2,1,0:T(8,128)S(1)}, u32[]{:S(2)}, u32[]{:S(2)}) collective-permute-start(f32[3,128,256]{2,1,0:T(8,128)S(1)} %slice.22.refs_7_.refs_11_.refs_15_), channel_id=1, source_target_pairs={{1,0},{2,3},{5,4},{6,7},{9,8},{10,11},{13,12},{14,15},{17,16},{18,... | collective-permute-start | bytes 1179656 | tf_op jit(solution)/shard_map/ppermute | solution.py:368
  82.1 10.6 %copy-start.5 = (f32[3,128,256]{2,1,0:T(8,128)}, f32[3,128,256]{2,1,0:T(8,128)S(1)}, u32[]{:S(2)}) copy-start(f32[3,128,256]{2,1,0:T(8,128)S(1)} %collective-permute-done.10.refs_19_.refs_23_.refs_27_) | copy-start | bytes 1179652
  83.0 10.6 %copy-start.11 = (s32[1,8,1,512]{3,2,1,0:T(1,128)S(1)}, s32[1,8,1,512]{3,2,1,0:T(1,128)}, u32[]{:S(2)}) copy-start(s32[1,8,1,512]{3,2,1,0:T(1,128)} %param.7) | copy-start | bytes 49156
  92.8 8.2 %copy-start.6 = (f32[3,128,256]{2,1,0:T(8,128)}, f32[3,128,256]{2,1,0:T(8,128)S(1)}, u32[]{:S(2)}) copy-start(f32[3,128,256]{2,1,0:T(8,128)S(1)} %collective-permute-done.16.refs_6_.refs_10_.refs_14_) | copy-start | bytes 1179652
  92.8 6.2 %collective-permute-start.17 = (f32[512,1024]{1,0:T(8,128)}, f32[512,1024]{1,0:T(8,128)S(1)}, u32[]{:S(2)}, u32[]{:S(2)}) collective-permute-start(f32[512,1024]{1,0:T(8,128)} %get-tuple-element.57.refs_1_), channel_id=1, source_target_pairs={{0,16},{16,0},{1,17},{17,1},{2,18},{18,2},{3,19},{19,3},{4,20},{20... | collective-permute-start | bytes 6291464 | tf_op jit(solution)/shard_map/ppermute | solution.py:411
  93.1 7.8 %collective-permute-start.15 = (f32[512,1024]{1,0:T(8,128)}, f32[512,1024]{1,0:T(8,128)}, u32[]{:S(2)}, u32[]{:S(2)}) collective-permute-start(f32[512,1024]{1,0:T(8,128)} %get-tuple-element.55.refs_0_), channel_id=1, source_target_pairs={{0,16},{16,0},{1,17},{17,1},{2,18},{18,2},{3,19},{19,3},{4,20},{20... | collective-permute-start | bytes 6291464 | tf_op jit(solution)/shard_map/ppermute | solution.py:408
  93.4 5.6 %collective-permute-start.19 = (f32[3,128,256]{2,1,0:T(8,128)S(1)}, f32[3,128,256]{2,1,0:T(8,128)S(1)}, u32[]{:S(2)}, u32[]{:S(2)}) collective-permute-start(f32[3,128,256]{2,1,0:T(8,128)S(1)} %collective-permute-done.16.refs_6_.refs_10_.refs_14_), channel_id=1, source_target_pairs={{0,16},{16,0},{1,17},{17,1},{2,18},{18,2},{3,19},{19,3},{4,20},{20... | collective-permute-start | bytes 1179656 | tf_op jit(solution)/shard_map/ppermute | solution.py:410
  93.7 5.3 %collective-permute-start.18 = (s32[8,4,128]{2,1,0:T(4,128)S(1)}, s32[8,4,128]{2,1,0:T(4,128)S(1)}, u32[]{:S(2)}, u32[]{:S(2)}) collective-permute-start(s32[8,4,128]{2,1,0:T(4,128)S(1)} %bitcast.20), channel_id=1, source_target_pairs={{0,16},{16,0},{1,17},{17,1},{2,18},{18,2},{3,19},{19,3},{4,20},{20... | collective-permute-start | bytes 49160 | tf_op jit(solution)/shard_map/ppermute | solution.py:349
  98.9 2.0 %copy-start.14 = (s32[8,4,128]{2,1,0:T(4,128)}, s32[8,4,128]{2,1,0:T(4,128)S(1)}, u32[]{:S(2)}) copy-start(s32[8,4,128]{2,1,0:T(4,128)S(1)} %collective-permute-done.18.refs_16_.refs_20_.refs_24_) | copy-start | bytes 49156
  98.9 2.0 %copy-start.7 = (f32[3,128,256]{2,1,0:T(8,128)}, f32[3,128,256]{2,1,0:T(8,128)S(1)}, u32[]{:S(2)}) copy-start(f32[3,128,256]{2,1,0:T(8,128)S(1)} %collective-permute-done.19.refs_18_.refs_22_.refs_26_) | copy-start | bytes 1179652
  (3 other events, 3.6 us)

commit v3 on v2

--- a/solution.py
+++ b/solution.py
@@ -183,21 +183,33 @@
 
         lax.fori_loop(0, group["count"], narrow, 0)
 
+    spans = []
+    for place, (_, count) in enumerate(plan["places"]):
+        slots = slots_ref[place, :, : count * part].astype(F32)
+        last = jnp.max(jnp.where(slots < row_count, slots, -1.0))
+        spans.append((jnp.min(slots).astype(jnp.int32), last.astype(jnp.int32)))
+
     def finish(block, carry):
         at = pl.ds(pl.multiple_of(block * rows, rows), rows)
         if bases:
             for n in range(len(bases)):
                 base_copy(n, block).wait()
             if plan["one_layer"]:
-                acc[at, :] = jnp.where(layer == 0, acc[at, :], 0.0)
+
+                @pl.when(layer != 0)
+                def _():
+                    acc[at, :] = jnp.zeros((rows, cols), F32)
+
             if len(bases) > 1:
                 acc[at, :] += sum(e[at, :] for e in extra)
         else:
             acc[at, :] = jnp.zeros((rows, cols), F32)
-        for place, (which, count) in enumerate(plan["places"]):
+        for place, (_, count) in enumerate(plan["places"]):
             used = count * part
 
-            @pl.when(ids[which] <= block)
+            low, high = spans[place]
+
+            @pl.when((low < (block + 1) * rows) & (high >= block * rows))
             def _(place=place, used=used):
                 hot = one_hot(slots_ref[place, :, :used], block * rows, rows)
                 acc[at, :] -= dot(hot, high_ref[place, :used]) + dot(hot, low_ref[place, :used])
@@ -321,48 +333,47 @@
     u_own = u_panels[0, :, 0]
     children = u_own.shape[0]
     first = children // 2
-    late = children * 3 // 8
+    late = children // 4
     rest, early = children - first, children - late
     row_map = l_map.reshape(children, 4, -1)
     col_map = u_map.reshape(children, 1, -1)
     swap = [(0, 1), (1, 0)]
     together = lax.optimization_barrier
 
-    quarter = first // 2
     pair = lax.ppermute(l_own, "col", ENDS)
     mid_b = lax.ppermute(l_own, "col", MIDDLE)
     by_x = lax.ppermute(u_own, "row", SWAP_X)
     by_y = lax.ppermute(u_own, "row", SWAP_Y)
-    pair, mid_b, by_x, by_y = together((pair, mid_b, by_x, by_y))
-
-    def diagonal(start):
-        cut = start + quarter
+    pair, by_x, by_y = together((pair, by_x, by_y))
+
+    def diagonal(start, count):
+        cut = start + count // 2
         return (
             lax.ppermute(by_x[start:cut], "row", SWAP_Y),
-            lax.ppermute(by_y[cut : start + first], "row", SWAP_X),
+            lax.ppermute(by_y[cut : start + count], "row", SWAP_X),
         )
 
-    by_xy1 = diagonal(0)
+    mid_a = lax.ppermute(mid_b, "col", OUTWARD)
     far_b = lax.ppermute(pair, "col", MIDDLE)
-    mid_a = lax.ppermute(mid_b, "col", OUTWARD)
-    by_xy2 = diagonal(first)
+    by_xy1 = diagonal(0, first)
+    by_xy2 = diagonal(first, rest)
     row_map_other = lax.ppermute(row_map, "gz", swap)
 
-    def near(base, start, u, chunks=(), groups=(), **options):
+    def near(base, start, count, u, chunks=(), groups=(), **options):
         group = dict(
-            count=first,
+            count=count,
             map=(row_map, start),
             col_map=(col_map, start),
             u=[(u_own, start), (by_x, start), (by_y, start)] + [(x, 0) for x in u],
-            cut=quarter,
+            cut=count // 2,
             chunks=[(0, 0, [(l_own, start)]), (1, 0, [(pair, start)]), *chunks],
         )
-        places = [(0, first), (1, first)] + [(2, children)] * len(chunks)
+        places = [(0, count), (1, count)] + [(2, children)] * len(chunks)
         return stage(shape, [base], places, [group, *groups], **options)
 
-    mine, *dense1 = near([front_matrix], 0, by_xy1, emit_sums=late, one_layer=True)
+    mine, *dense1 = near([front_matrix], 0, first, by_xy1, emit_sums=late, one_layer=True)
     dense1, sums = dense1[:2], dense1[2:]
-    far_b, mine = together((far_b, mine))
+    far_b, mid_a, mine = together((far_b, mid_a, mine))
     far_b2, far_b1 = far_b[:late], far_b[late:]
     far_a1 = lax.ppermute(far_b1, "col", OUTWARD)
     far_a2 = lax.ppermute(far_b2, "col", OUTWARD)
@@ -372,6 +383,7 @@
     mine, *dense2 = near(
         [mine],
         first,
+        rest,
         (by_xy2a, by_xy2b),
         [(2, first, [(mid_a, first), (mid_b, first)])],
         [

time: 114 us -> 108 us (0.947)
  the two profiles are of different devices: /device:TPU:19 before, /device:TPU:0 now
where the time goes in v3:
time: 108 us; the launch traced here: 107 us
  Pallas kernels  45.7 us (42%)
  waiting for transfers between devices  37.9 us (35%)
  starting transfers between devices  18 us (17%)
  local copies, waits for them, and re-layouts  5.22 us (5%)
    pallas_call x4, Pallas kernels, stage(): pl.pallas_call(functools.partial(stage_kernel, plan), in_specs=[pl.BlockS...  45.7 us
    ppermute x1, waiting for transfers between devices, four_by_four(): pair = lax.ppermute(l_own, 'col', ENDS)  18.7 us
    ppermute x1, waiting for transfers between devices, four_by_four(): row_map_other = lax.ppermute(row_map, 'gz', swap)  6.15 us
    ppermute x2, waiting for transfers between devices, diagonal(): lax.ppermute(by_x[start:cut], 'row', SWAP_Y)  5.95 us
    ppermute x1, starting transfers between devices, four_by_four(): pair = lax.ppermute(l_own, 'col', ENDS)  3.02 us
    ppermute x1, waiting for transfers between devices, four_by_four(): far_a1 = lax.ppermute(far_b1, 'col', OUTWARD)  2.69 us
    unnamed x30, local copies, waits for them, and re-layouts  2.28 us
    slice x2, local copies, waits for them, and re-layouts, four_by_four(): far_b2, far_b1 = (far_b[:late], far_b[late:])  2.17 us
  transfers between devices with their start and end apart: 19, of which 9 were waited for; matrix products, arithmetic and copies ran while one was open for 3% of the time, Pallas kernels for 35%

profile of v3, /device:TPU:0, one launch (start us, length us, event | category | flops | bytes accessed | tf_op | source)
XLA Modules:
  0.0 107.1 jit_solution(14646381283496761255)
XLA Ops:
  0.0 3.0 %collective-permute-start = (f32[8,128,256]{2,1,0:T(8,128)}, f32[8,128,256]{2,1,0:T(8,128)S(1)}, u32[]{:S(2)}, u32[]{:S(2)}) collective-permute-start(f32[8,128,256]{2,1,0:T(8,128)} %bitcast.8), channel_id=1, source_target_pairs={{0,1},{1,0},{2,3},{3,2},{4,5},{5,4},{6,7},{7,6},{8,9},{9,8},{10,11... | collective-permute-start | bytes 3145736 | tf_op jit(solution)/shard_map/ppermute | solution.py:343
  3.0 1.5 %collective-permute-start.1 = (f32[8,128,256]{2,1,0:T(8,128)}, f32[8,128,256]{2,1,0:T(8,128)S(1)}, u32[]{:S(2)}, u32[]{:S(2)}) collective-permute-start(f32[8,128,256]{2,1,0:T(8,128)} %bitcast.4), channel_id=1, source_target_pairs={{0,4},{4,0},{8,12},{12,8},{1,5},{5,1},{9,13},{13,9},{2,6},{6,2},{1... | collective-permute-start | bytes 3145736 | tf_op jit(solution)/shard_map/ppermute | solution.py:345
  4.5 1.5 %collective-permute-start.2 = (f32[8,128,256]{2,1,0:T(8,128)}, f32[8,128,256]{2,1,0:T(8,128)S(1)}, u32[]{:S(2)}, u32[]{:S(2)}) collective-permute-start(f32[8,128,256]{2,1,0:T(8,128)} %bitcast.5), channel_id=1, source_target_pairs={{0,8},{8,0},{4,12},{12,4},{1,9},{9,1},{5,13},{13,5},{2,10},{10,2},... | collective-permute-start | bytes 3145736 | tf_op jit(solution)/shard_map/ppermute | solution.py:346
  6.0 1.7 %collective-permute-start.4 = (f32[8,128,256]{2,1,0:T(8,128)}, f32[8,128,256]{2,1,0:T(8,128)}, u32[]{:S(2)}, u32[]{:S(2)}) collective-permute-start(f32[8,128,256]{2,1,0:T(8,128)} %bitcast.9), channel_id=1, source_target_pairs={{1,2},{2,1},{5,6},{6,5},{9,10},{10,9},{13,14},{14,13},{17,18},{18,... | collective-permute-start | bytes 3145736 | tf_op jit(solution)/shard_map/ppermute | solution.py:344
  7.7 18.7 %collective-permute-done.refs_9_ = f32[8,128,256]{2,1,0:T(8,128)S(1)} collective-permute-done((f32[8,128,256]{2,1,0:T(8,128)}, f32[8,128,256]{2,1,0:T(8,128)S(1)}, u32[]{:S(2)}, u32[]{:S(2)}) %collective-permute-start) | collective-permute-done | bytes 1048608 | tf_op jit(solution)/shard_map/ppermute | solution.py:343
  26.4 1.5 %collective-permute-done.1.refs_4_ = f32[8,128,256]{2,1,0:T(8,128)S(1)} collective-permute-done((f32[8,128,256]{2,1,0:T(8,128)}, f32[8,128,256]{2,1,0:T(8,128)S(1)}, u32[]{:S(2)}, u32[]{:S(2)}) %collective-permute-start.1) | collective-permute-done | bytes 1048608 | tf_op jit(solution)/shard_map/ppermute | solution.py:345
  27.9 1.2 %collective-permute-done.2.refs_5_ = f32[8,128,256]{2,1,0:T(8,128)S(1)} collective-permute-done((f32[8,128,256]{2,1,0:T(8,128)}, f32[8,128,256]{2,1,0:T(8,128)S(1)}, u32[]{:S(2)}, u32[]{:S(2)}) %collective-permute-start.2) | collective-permute-done | bytes 1048608 | tf_op jit(solution)/shard_map/ppermute | solution.py:346
  29.1 1.6 %collective-permute-start.3 = (f32[8,128,256]{2,1,0:T(8,128)S(1)}, f32[8,128,256]{2,1,0:T(8,128)}, u32[]{:S(2)}, u32[]{:S(2)}) collective-permute-start(f32[8,128,256]{2,1,0:T(8,128)S(1)} %collective-permute-done.refs_9_), channel_id=1, source_target_pairs={{1,2},{2,1},{5,6},{6,5},{9,10},{10,9},{13,14},{14,13},{17,18},{18,... | collective-permute-start | bytes 3145736 | tf_op jit(solution)/shard_map/ppermute | solution.py:357
  30.7 1.3 %collective-permute-start.5 = (f32[8,128,256]{2,1,0:T(8,128)}, f32[8,128,256]{2,1,0:T(8,128)}, u32[]{:S(2)}, u32[]{:S(2)}) collective-permute-start(f32[8,128,256]{2,1,0:T(8,128)} %collective-permute-done.4.refs_11_.refs_16_), channel_id=1, source_target_pairs={{1,0},{2,3},{5,4},{6,7},{9,8},{10,11},{13,12},{14,15},{17,16},{18,... | collective-permute-start | bytes 3145736 | tf_op jit(solution)/shard_map/ppermute | solution.py:356
  32.0 1.6 %collective-permute-start.6 = (f32[2,128,256]{2,1,0:T(8,128)S(1)}, f32[2,128,256]{2,1,0:T(8,128)S(1)}, u32[]{:S(2)}, u32[]{:S(2)}) collective-permute-start(f32[2,128,256]{2,1,0:T(8,128)S(1)} %get-tuple-element.60), channel_id=1, source_target_pairs={{0,8},{8,0},{4,12},{12,4},{1,9},{9,1},{5,13},{13,5},{2,10},{10,2},... | collective-permute-start | bytes 786440 | tf_op jit(solution)/shard_map/ppermute | solution.py:352
  33.6 0.7 fusion
  34.3 0.5 collective-permute-start.7
  34.9 0.5 collective-permute-start.8
  35.4 5.9 %collective-permute-done.6.refs_6_ = f32[2,128,256]{2,1,0:T(8,128)S(1)} collective-permute-done((f32[2,128,256]{2,1,0:T(8,128)S(1)}, f32[2,128,256]{2,1,0:T(8,128)S(1)}, u32[]{:S(2)}, u32[]{:S(2)}) %collective-permute-start.6) | collective-permute-done | bytes 262176 | tf_op jit(solution)/shard_map/ppermute | solution.py:352
  41.3 0.5 collective-permute-start.9
  41.8 0.7 collective-permute-done.7.refs_7_
  42.6 0.7 copy-done.13
  43.3 13.0 %shard_map.55 = (f32[1024,1024]{1,0:T(8,128)}, bf16[4,1024,256]{2,1,0:T(8,128)(2,1)}, bf16[4,1024,256]{2,1,0:T(8,128)(2,1)}, f32[1,1024,256]{2,1,0:T(8,128)}, f32[1,1024,256]{2,1,0:T(8,128)}) custom-call(f32[1024,1024]{1,0:T(8,128)} %refs_0_.1, s32[8,4,128]{2,1,0:T(4,128)} %bitcast.12, s32[8,1,512]{2,1,0:T(1,128)} %bitcast.20, f32[8,128,256]{2,1,0:T(8,128)} %bitcast.6, ...), custom_call_target="tpu_custom_call" | custom-call | flops 1000 | bytes 1000 | tf_op jit(solution)/shard_map/pallas_call | solution.py:306
  56.4 0.5 collective-permute-start.12
  57.2 1.2 %slice.23.refs_5_.refs_10_ = f32[6,128,256]{2,1,0:T(8,128)S(1)} slice(f32[8,128,256]{2,1,0:T(8,128)} %collective-permute-done.3), slice={[2:8], [0:128], [0:256]} | slice | bytes 1572864 | tf_op jit(solution)/shard_map/slice | solution.py:377
  58.5 1.3 %collective-permute-start.13 = (f32[6,128,256]{2,1,0:T(8,128)S(1)}, f32[6,128,256]{2,1,0:T(8,128)S(1)}, u32[]{:S(2)}, u32[]{:S(2)}) collective-permute-start(f32[6,128,256]{2,1,0:T(8,128)S(1)} %slice.23.refs_5_.refs_10_), channel_id=1, source_target_pairs={{1,0},{2,3},{5,4},{6,7},{9,8},{10,11},{13,12},{14,15},{17,16},{18,... | collective-permute-start | bytes 2359304 | tf_op jit(solution)/shard_map/ppermute | solution.py:378
  59.8 1.0 slice.22.refs_7_.refs_11_
  60.8 1.3 %collective-permute-start.15 = (f32[2,128,256]{2,1,0:T(8,128)S(1)}, f32[2,128,256]{2,1,0:T(8,128)S(1)}, u32[]{:S(2)}, u32[]{:S(2)}) collective-permute-start(f32[2,128,256]{2,1,0:T(8,128)S(1)} %slice.22.refs_7_.refs_11_), channel_id=1, source_target_pairs={{1,0},{2,3},{5,4},{6,7},{9,8},{10,11},{13,12},{14,15},{17,16},{18,... | collective-permute-start | bytes 786440 | tf_op jit(solution)/shard_map/ppermute | solution.py:379
  62.1 17.5 %shard_map.56 = (f32[1024,1024]{1,0:T(8,128)}, bf16[4,1024,256]{2,1,0:T(8,128)(2,1)}, bf16[4,1024,256]{2,1,0:T(8,128)(2,1)}) custom-call(f32[1024,1024]{1,0:T(8,128)} %get-tuple-element.35.refs_0_, s32[8,4,128]{2,1,0:T(4,128)} %bitcast.13, s32[8,1,512]{2,1,0:T(1,128)} %bitcast.21, f32[8,128,256]{2,1,0:T(8,128)} %bitcast.7, f32[8,128,256]{2,1,0:T(8,128)} %copy-done.1, ...), custom_call_target="tpu_custom_call" | custom-call | flops 1000 | bytes 1000 | tf_op jit(solution)/shard_map/pallas_call | solution.py:306
  79.7 2.7 %collective-permute-done.13.refs_4_.refs_9_ = f32[6,128,256]{2,1,0:T(8,128)S(1)} collective-permute-done((f32[6,128,256]{2,1,0:T(8,128)S(1)}, f32[6,128,256]{2,1,0:T(8,128)S(1)}, u32[]{:S(2)}, u32[]{:S(2)}) %collective-permute-start.13) | collective-permute-done | bytes 786464 | tf_op jit(solution)/shard_map/ppermute | solution.py:378
  82.4 0.9 copy-done.4
  83.2 7.2 %shard_map.57 = (f32[512,1024]{1,0:T(8,128)}, f32[512,1024]{1,0:T(8,128)}) custom-call(f32[1024,1024]{1,0:T(8,128)} %get-tuple-element.47.refs_0_, s32[8,4,128]{2,1,0:T(4,128)} %bitcast.15, bf16[4,1024,256]{2,1,0:T(8,128)(2,1)} %get-tuple-element.41.refs_13_.refs_2_, bf16[4,1024,256]{2,1,0:T(8,128)(2,1)} %get-tuple-element.42.refs_14_.refs_3_, ...), custom_call_target="tpu_custom_call" | custom-call | flops 1000 | bytes 1000 | tf_op jit(solution)/shard_map/pallas_call | solution.py:306
  90.6 0.5 collective-permute-start.14
  91.6 6.1 %collective-permute-done.17.refs_12_.refs_16_ = s32[8,4,128]{2,1,0:T(4,128)S(1)} collective-permute-done((s32[8,4,128]{2,1,0:T(4,128)S(1)}, s32[8,4,128]{2,1,0:T(4,128)S(1)}, u32[]{:S(2)}, u32[]{:S(2)}) %collective-permute-start.17) | collective-permute-done | bytes 16416 | tf_op jit(solution)/shard_map/ppermute | solution.py:360
  97.8 0.7 collective-permute-done.14.refs_2_
  98.5 0.7 copy-done.6
  99.2 7.9 %shard_map.58 = f32[1024,1024]{1,0:T(8,128)} custom-call(f32[512,1024]{1,0:T(8,128)} %get-tuple-element.50.refs_0_, f32[512,1024]{1,0:T(8,128)} %get-tuple-element.52.refs_1_, f32[512,1024]{1,0:T(8,128)} %collective-permute-done.14.refs_2_, f32[512,1024]{1,0:T(8,128)} %copy-done.6, s32[8,4,128]{2,1,0:T(4,128)} %bitcast.17, ...), custom_call_target="tpu_custom_call" | custom-call | flops 1000 | bytes 1000 | tf_op jit(solution)/shard_map/pallas_call | solution.py:306
  (44 shorter events, 1.2 us)
Async XLA Ops:
  0.0 26.4 %collective-permute-start = (f32[8,128,256]{2,1,0:T(8,128)}, f32[8,128,256]{2,1,0:T(8,128)S(1)}, u32[]{:S(2)}, u32[]{:S(2)}) collective-permute-start(f32[8,128,256]{2,1,0:T(8,128)} %bitcast.8), channel_id=1, source_target_pairs={{0,1},{1,0},{2,3},{3,2},{4,5},{5,4},{6,7},{7,6},{8,9},{9,8},{10,11... | collective-permute-start | bytes 3145736 | tf_op jit(solution)/shard_map/ppermute | solution.py:343
  3.0 24.8 %collective-permute-start.1 = (f32[8,128,256]{2,1,0:T(8,128)}, f32[8,128,256]{2,1,0:T(8,128)S(1)}, u32[]{:S(2)}, u32[]{:S(2)}) collective-permute-start(f32[8,128,256]{2,1,0:T(8,128)} %bitcast.4), channel_id=1, source_target_pairs={{0,4},{4,0},{8,12},{12,8},{1,5},{5,1},{9,13},{13,9},{2,6},{6,2},{1... | collective-permute-start | bytes 3145736 | tf_op jit(solution)/shard_map/ppermute | solution.py:345
  4.5 24.5 %collective-permute-start.2 = (f32[8,128,256]{2,1,0:T(8,128)}, f32[8,128,256]{2,1,0:T(8,128)S(1)}, u32[]{:S(2)}, u32[]{:S(2)}) collective-permute-start(f32[8,128,256]{2,1,0:T(8,128)} %bitcast.5), channel_id=1, source_target_pairs={{0,8},{8,0},{4,12},{12,4},{1,9},{9,1},{5,13},{13,5},{2,10},{10,2},... | collective-permute-start | bytes 3145736 | tf_op jit(solution)/shard_map/ppermute | solution.py:346
  6.0 24.7 %collective-permute-start.4 = (f32[8,128,256]{2,1,0:T(8,128)}, f32[8,128,256]{2,1,0:T(8,128)}, u32[]{:S(2)}, u32[]{:S(2)}) collective-permute-start(f32[8,128,256]{2,1,0:T(8,128)} %bitcast.9), channel_id=1, source_target_pairs={{1,2},{2,1},{5,6},{6,5},{9,10},{10,9},{13,14},{14,13},{17,18},{18,... | collective-permute-start | bytes 3145736 | tf_op jit(solution)/shard_map/ppermute | solution.py:344
  26.4 16.2 %copy-start.3 = (f32[8,128,256]{2,1,0:T(8,128)}, f32[8,128,256]{2,1,0:T(8,128)S(1)}, u32[]{:S(2)}) copy-start(f32[8,128,256]{2,1,0:T(8,128)S(1)} %collective-permute-done.refs_9_) | copy-start | bytes 3145732
  27.9 14.7 %copy-start.1 = (f32[8,128,256]{2,1,0:T(8,128)}, f32[8,128,256]{2,1,0:T(8,128)S(1)}, u32[]{:S(2)}) copy-start(f32[8,128,256]{2,1,0:T(8,128)S(1)} %collective-permute-done.1.refs_4_) | copy-start | bytes 3145732
  29.1 13.5 %copy-start.2 = (f32[8,128,256]{2,1,0:T(8,128)}, f32[8,128,256]{2,1,0:T(8,128)S(1)}, u32[]{:S(2)}) copy-start(f32[8,128,256]{2,1,0:T(8,128)S(1)} %collective-permute-done.2.refs_5_) | copy-start | bytes 3145732
  29.1 27.8 %collective-permute-start.3 = (f32[8,128,256]{2,1,0:T(8,128)S(1)}, f32[8,128,256]{2,1,0:T(8,128)}, u32[]{:S(2)}, u32[]{:S(2)}) collective-permute-start(f32[8,128,256]{2,1,0:T(8,128)S(1)} %collective-permute-done.refs_9_), channel_id=1, source_target_pairs={{1,2},{2,1},{5,6},{6,5},{9,10},{10,9},{13,14},{14,13},{17,18},{18,... | collective-permute-start | bytes 3145736 | tf_op jit(solution)/shard_map/ppermute | solution.py:357
  30.7 26.5 %collective-permute-start.5 = (f32[8,128,256]{2,1,0:T(8,128)}, f32[8,128,256]{2,1,0:T(8,128)}, u32[]{:S(2)}, u32[]{:S(2)}) collective-permute-start(f32[8,128,256]{2,1,0:T(8,128)} %collective-permute-done.4.refs_11_.refs_16_), channel_id=1, source_target_pairs={{1,0},{2,3},{5,4},{6,7},{9,8},{10,11},{13,12},{14,15},{17,16},{18,... | collective-permute-start | bytes 3145736 | tf_op jit(solution)/shard_map/ppermute | solution.py:356
  32.0 9.3 %collective-permute-start.6 = (f32[2,128,256]{2,1,0:T(8,128)S(1)}, f32[2,128,256]{2,1,0:T(8,128)S(1)}, u32[]{:S(2)}, u32[]{:S(2)}) collective-permute-start(f32[2,128,256]{2,1,0:T(8,128)S(1)} %get-tuple-element.60), channel_id=1, source_target_pairs={{0,8},{8,0},{4,12},{12,4},{1,9},{9,1},{5,13},{13,5},{2,10},{10,2},... | collective-permute-start | bytes 786440 | tf_op jit(solution)/shard_map/ppermute | solution.py:352
  34.3 8.2 %collective-permute-start.7 = (f32[2,128,256]{2,1,0:T(8,128)S(1)}, f32[2,128,256]{2,1,0:T(8,128)S(1)}, u32[]{:S(2)}, u32[]{:S(2)}) collective-permute-start(f32[2,128,256]{2,1,0:T(8,128)S(1)} %get-tuple-element.58), channel_id=1, source_target_pairs={{0,4},{4,0},{8,12},{12,8},{1,5},{5,1},{9,13},{13,9},{2,6},{6,2},{1... | collective-permute-start | bytes 786440 | tf_op jit(solution)/shard_map/ppermute | solution.py:353
  34.9 21.4 %collective-permute-start.8 = (f32[2,128,256]{2,1,0:T(8,128)S(1)}, f32[2,128,256]{2,1,0:T(8,128)}, u32[]{:S(2)}, u32[]{:S(2)}) collective-permute-start(f32[2,128,256]{2,1,0:T(8,128)S(1)} %get-tuple-element.59), channel_id=1, source_target_pairs={{0,8},{8,0},{4,12},{12,4},{1,9},{9,1},{5,13},{13,5},{2,10},{10,2},... | collective-permute-start | bytes 786440 | tf_op jit(solution)/shard_map/ppermute | solution.py:352
  41.3 1.2 %copy-start.12 = (f32[2,128,256]{2,1,0:T(8,128)}, f32[2,128,256]{2,1,0:T(8,128)S(1)}, u32[]{:S(2)}) copy-start(f32[2,128,256]{2,1,0:T(8,128)S(1)} %collective-permute-done.6.refs_6_) | copy-start | bytes 786436
  41.3 15.0 %collective-permute-start.9 = (f32[2,128,256]{2,1,0:T(8,128)}, f32[2,128,256]{2,1,0:T(8,128)}, u32[]{:S(2)}, u32[]{:S(2)}) collective-permute-start(f32[2,128,256]{2,1,0:T(8,128)} %get-tuple-element.57), channel_id=1, source_target_pairs={{0,4},{4,0},{8,12},{12,8},{1,5},{5,1},{9,13},{13,9},{2,6},{6,2},{1... | collective-permute-start | bytes 786440 | tf_op jit(solution)/shard_map/ppermute | solution.py:353
  56.3 23.3 %collective-permute-start.11 = (f32[1,1024,256]{2,1,0:T(8,128)}, f32[1,1024,256]{2,1,0:T(8,128)S(1)}, u32[]{:S(2)}, u32[]{:S(2)}) collective-permute-start(f32[1,1024,256]{2,1,0:T(8,128)} %get-tuple-element.45.refs_5_), channel_id=1, source_target_pairs={{0,16},{16,0},{1,17},{17,1},{2,18},{18,2},{3,19},{19,3},{4,20},{20... | collective-permute-start | bytes 3145736 | tf_op jit(solution)/shard_map/ppermute | solution.py:382
  56.4 23.2 %collective-permute-start.12 = (f32[1,1024,256]{2,1,0:T(8,128)}, f32[1,1024,256]{2,1,0:T(8,128)}, u32[]{:S(2)}, u32[]{:S(2)}) collective-permute-start(f32[1,1024,256]{2,1,0:T(8,128)} %get-tuple-element.46.refs_9_), channel_id=1, source_target_pairs={{0,16},{16,0},{1,17},{17,1},{2,18},{18,2},{3,19},{19,3},{4,20},{20... | collective-permute-start | bytes 3145736 | tf_op jit(solution)/shard_map/ppermute | solution.py:382
  58.4 21.2 %copy-start = (f32[6,128,256]{2,1,0:T(8,128)}, f32[6,128,256]{2,1,0:T(8,128)S(1)}, u32[]{:S(2)}) copy-start(f32[6,128,256]{2,1,0:T(8,128)S(1)} %slice.23.refs_5_.refs_10_) | copy-start | bytes 2359300
  58.5 23.9 %collective-permute-start.13 = (f32[6,128,256]{2,1,0:T(8,128)S(1)}, f32[6,128,256]{2,1,0:T(8,128)S(1)}, u32[]{:S(2)}, u32[]{:S(2)}) collective-permute-start(f32[6,128,256]{2,1,0:T(8,128)S(1)} %slice.23.refs_5_.refs_10_), channel_id=1, source_target_pairs={{1,0},{2,3},{5,4},{6,7},{9,8},{10,11},{13,12},{14,15},{17,16},{18,... | collective-permute-start | bytes 2359304 | tf_op jit(solution)/shard_map/ppermute | solution.py:378
  60.7 18.9 %copy-start.5 = (f32[2,128,256]{2,1,0:T(8,128)}, f32[2,128,256]{2,1,0:T(8,128)S(1)}, u32[]{:S(2)}) copy-start(f32[2,128,256]{2,1,0:T(8,128)S(1)} %slice.22.refs_7_.refs_11_) | copy-start | bytes 786436
  60.7 18.9 %collective-permute-start.10 = (f32[2,128,256]{2,1,0:T(8,128)S(1)}, f32[2,128,256]{2,1,0:T(8,128)S(1)}, u32[]{:S(2)}, u32[]{:S(2)}) collective-permute-start(f32[2,128,256]{2,1,0:T(8,128)S(1)} %slice.22.refs_7_.refs_11_), channel_id=1, source_target_pairs={{0,16},{16,0},{1,17},{17,1},{2,18},{18,2},{3,19},{19,3},{4,20},{20... | collective-permute-start | bytes 786440 | tf_op jit(solution)/shard_map/ppermute | solution.py:380
  60.8 29.7 %collective-permute-start.15 = (f32[2,128,256]{2,1,0:T(8,128)S(1)}, f32[2,128,256]{2,1,0:T(8,128)S(1)}, u32[]{:S(2)}, u32[]{:S(2)}) collective-permute-start(f32[2,128,256]{2,1,0:T(8,128)S(1)} %slice.22.refs_7_.refs_11_), channel_id=1, source_target_pairs={{1,0},{2,3},{5,4},{6,7},{9,8},{10,11},{13,12},{14,15},{17,16},{18,... | collective-permute-start | bytes 786440 | tf_op jit(solution)/shard_map/ppermute | solution.py:379
  79.6 10.8 %copy-start.10 = (f32[1,1024,256]{2,1,0:T(8,128)}, f32[1,1024,256]{2,1,0:T(8,128)S(1)}, u32[]{:S(2)}) copy-start(f32[1,1024,256]{2,1,0:T(8,128)S(1)} %collective-permute-done.11.refs_13_) | copy-start | bytes 3145732
  79.7 10.8 %copy-start.7 = (f32[2,128,256]{2,1,0:T(8,128)}, f32[2,128,256]{2,1,0:T(8,128)S(1)}, u32[]{:S(2)}) copy-start(f32[2,128,256]{2,1,0:T(8,128)S(1)} %collective-permute-done.10.refs_15_.refs_19_) | copy-start | bytes 786436
  82.4 0.9 copy-start.4
  83.2 7.9 %copy-start.11 = (s32[1,8,1,512]{3,2,1,0:T(1,128)S(1)}, s32[1,8,1,512]{3,2,1,0:T(1,128)}, u32[]{:S(2)}) copy-start(s32[1,8,1,512]{3,2,1,0:T(1,128)} %param.7) | copy-start | bytes 49156
  90.5 8.0 %copy-start.8 = (f32[2,128,256]{2,1,0:T(8,128)}, f32[2,128,256]{2,1,0:T(8,128)S(1)}, u32[]{:S(2)}) copy-start(f32[2,128,256]{2,1,0:T(8,128)S(1)} %collective-permute-done.15.refs_6_.refs_10_) | copy-start | bytes 786436
  90.5 7.2 %collective-permute-start.16 = (f32[512,1024]{1,0:T(8,128)}, f32[512,1024]{1,0:T(8,128)S(1)}, u32[]{:S(2)}, u32[]{:S(2)}) collective-permute-start(f32[512,1024]{1,0:T(8,128)} %get-tuple-element.52.refs_1_), channel_id=1, source_target_pairs={{0,16},{16,0},{1,17},{17,1},{2,18},{18,2},{3,19},{19,3},{4,20},{20... | collective-permute-start | bytes 6291464 | tf_op jit(solution)/shard_map/ppermute | solution.py:423
  90.6 7.9 %collective-permute-start.14 = (f32[512,1024]{1,0:T(8,128)}, f32[512,1024]{1,0:T(8,128)}, u32[]{:S(2)}, u32[]{:S(2)}) collective-permute-start(f32[512,1024]{1,0:T(8,128)} %get-tuple-element.50.refs_0_), channel_id=1, source_target_pairs={{0,16},{16,0},{1,17},{17,1},{2,18},{18,2},{3,19},{19,3},{4,20},{20... | collective-permute-start | bytes 6291464 | tf_op jit(solution)/shard_map/ppermute | solution.py:420
  91.1 6.7 %collective-permute-start.18 = (f32[2,128,256]{2,1,0:T(8,128)S(1)}, f32[2,128,256]{2,1,0:T(8,128)S(1)}, u32[]{:S(2)}, u32[]{:S(2)}) collective-permute-start(f32[2,128,256]{2,1,0:T(8,128)S(1)} %collective-permute-done.15.refs_6_.refs_10_), channel_id=1, source_target_pairs={{0,16},{16,0},{1,17},{17,1},{2,18},{18,2},{3,19},{19,3},{4,20},{20... | collective-permute-start | bytes 786440 | tf_op jit(solution)/shard_map/ppermute | solution.py:422
  91.2 6.6 %collective-permute-start.17 = (s32[8,4,128]{2,1,0:T(4,128)S(1)}, s32[8,4,128]{2,1,0:T(4,128)S(1)}, u32[]{:S(2)}, u32[]{:S(2)}) collective-permute-start(s32[8,4,128]{2,1,0:T(4,128)S(1)} %bitcast.19), channel_id=1, source_target_pairs={{0,16},{16,0},{1,17},{17,1},{2,18},{18,2},{3,19},{19,3},{4,20},{20... | collective-permute-start | bytes 49160 | tf_op jit(solution)/shard_map/ppermute | solution.py:360
  97.7 0.7 copy-start.14
  97.8 1.4 %copy-start.6 = (f32[512,1024]{1,0:T(8,128)}, f32[512,1024]{1,0:T(8,128)S(1)}, u32[]{:S(2)}) copy-start(f32[512,1024]{1,0:T(8,128)S(1)} %collective-permute-done.16.refs_3_) | copy-start | bytes 6291460
  (2 other events, 1.4 us)

commit v4 on v3

--- a/solution.py
+++ b/solution.py
@@ -118,7 +118,7 @@
             whole(i).start()
     for group in plan["groups"]:
         for child in range(group["count"]):
-            for i in group["dense"]:
+            for i in group["each"]:
                 one(i, child).start()
     for block in range(blocks):
         for n, pieces in enumerate(bases):
@@ -131,6 +131,8 @@
     for group in plan["groups"]:
 
         def narrow(child, carry, group=group):
+            for i in group["each"]:
+                one(i, child).wait()
             if "u" in group:
                 panels = [held[i][child] for i in group["u"][:3]]
                 far_a, far_b = (held[i] for i in group["u"][3:])
@@ -158,13 +160,10 @@
                         staged[2 + c][0] = full_high + full_low
                         dense_copy(2 + c, 0).start()
 
+            elif len(group["dense"]) == 2:
+                dense_high, dense_low = (held[i][child] for i in group["dense"])
             else:
-                for i in group["dense"]:
-                    one(i, child).wait()
-                if len(group["dense"]) == 2:
-                    dense_high, dense_low = (held[i][child] for i in group["dense"])
-                else:
-                    dense_high, dense_low = split(held[group["dense"][0]][child])
+                dense_high, dense_low = split(held[group["dense"][0]][child])
             panels = []
             for place, first, which, members in group["chunks"]:
                 panels.append(sum(held[m][child] for m in members))
@@ -236,7 +235,7 @@
     for base in bases:
         base_at.append(list(range(len(inputs), len(inputs) + len(base))))
         inputs += base
-    held, ranges, single, layout = [], {}, [], []
+    held, ranges, single, kept, layout = [], {}, [], [], []
 
     def take(pair, count):
         array, first = pair
@@ -254,14 +253,19 @@
         if "u" in g:
             item["col_map"] = take(g["col_map"], count)
             item["u"] = [take(p, count) for p in g["u"]]
+            item["each"] = item["u"][:3]
             item["cut"] = g["cut"]
         else:
             item["dense"] = [take(p, count) for p in g["dense"]]
-            single += item["dense"]
+            kept += item["dense"]
+            item["each"] = list(item["dense"])
         item["chunks"] = [
             (place, first, places[place][0], [take(p, count) for p in panels])
             for place, first, panels in g["chunks"]
         ]
+        for _, _, _, members in item["chunks"]:
+            item["each"] += members
+        single += item["each"]
         part, depth = g["chunks"][0][2][0][0].shape[1:]
         layout.append(item)
     rows = 2 * part
@@ -290,7 +294,6 @@
     )
     deepest = max(g["count"] for g in groups)
     blocks = row_count // rows
-    kept = set(single)
     buffers = (
         [((ranges[i][1],) + inputs[i].shape[1:], inputs[i].dtype) for i in held]
         + [

time: 108 us -> 106 us (0.981)
  Pallas kernels: 45.7 us -> 43.7 us
    pallas_call x4, Pallas kernels: 45.7 us -> 43.7 us  [stage(): pl.pallas_call(functools.partial(stage_kernel, plan), in_specs=[pl.BlockS...]
    ppermute x1, waiting for transfers between devices: 0.32 us -> 1.47 us  [four_by_four(): mid_a = lax.ppermute(mid_b, 'col', OUTWARD)]
  transfers between devices with their start and end apart: 19 -> 19, of which waited for: 9 -> 9; matrix products, arithmetic and copies ran while one was open for 3% -> 3% of each run, Pallas kernels for 35% -> 34%
where the time goes in v4:
time: 106 us
  Pallas kernels  43.7 us (41%)
  waiting for transfers between devices  38.3 us (36%)
  starting transfers between devices  18 us (17%)
  local copies, waits for them, and re-layouts  5.22 us (5%)
    pallas_call x4, Pallas kernels, stage(): pl.pallas_call(functools.partial(stage_kernel, plan), in_specs=[pl.BlockS...  43.7 us
    ppermute x1, waiting for transfers between devices, four_by_four(): pair = lax.ppermute(l_own, 'col', ENDS)  18.7 us
    ppermute x1, waiting for transfers between devices, four_by_four(): row_map_other = lax.ppermute(row_map, 'gz', swap)  6.15 us
    ppermute x2, waiting for transfers between devices, diagonal(): lax.ppermute(by_x[start:cut], 'row', SWAP_Y)  5.95 us
    ppermute x1, starting transfers between devices, four_by_four(): pair = lax.ppermute(l_own, 'col', ENDS)  3.02 us
    unnamed x30, local copies, waits for them, and re-layouts  2.28 us
    slice x2, local copies, waits for them, and re-layouts, four_by_four(): far_b2, far_b1 = (far_b[:late], far_b[late:])  2.17 us
  transfers between devices with their start and end apart: 19, of which 9 were waited for; matrix products, arithmetic and copies ran while one was open for 3% of the time, Pallas kernels for 34%

profile of v4, /device:TPU:0, one launch (start us, length us, event | category | flops | bytes accessed | tf_op | source)
XLA Modules:
  0.0 105.6 jit_solution(16826662419437716419)
XLA Ops:
  0.0 3.0 %collective-permute-start = (f32[8,128,256]{2,1,0:T(8,128)}, f32[8,128,256]{2,1,0:T(8,128)S(1)}, u32[]{:S(2)}, u32[]{:S(2)}) collective-permute-start(f32[8,128,256]{2,1,0:T(8,128)} %bitcast.8), channel_id=1, source_target_pairs={{0,1},{1,0},{2,3},{3,2},{4,5},{5,4},{6,7},{7,6},{8,9},{9,8},{10,11... | collective-permute-start | bytes 3145736 | tf_op jit(solution)/shard_map/ppermute | solution.py:346
  3.0 1.5 %collective-permute-start.1 = (f32[8,128,256]{2,1,0:T(8,128)}, f32[8,128,256]{2,1,0:T(8,128)S(1)}, u32[]{:S(2)}, u32[]{:S(2)}) collective-permute-start(f32[8,128,256]{2,1,0:T(8,128)} %bitcast.4), channel_id=1, source_target_pairs={{0,4},{4,0},{8,12},{12,8},{1,5},{5,1},{9,13},{13,9},{2,6},{6,2},{1... | collective-permute-start | bytes 3145736 | tf_op jit(solution)/shard_map/ppermute | solution.py:348
  4.5 1.5 %collective-permute-start.2 = (f32[8,128,256]{2,1,0:T(8,128)}, f32[8,128,256]{2,1,0:T(8,128)S(1)}, u32[]{:S(2)}, u32[]{:S(2)}) collective-permute-start(f32[8,128,256]{2,1,0:T(8,128)} %bitcast.5), channel_id=1, source_target_pairs={{0,8},{8,0},{4,12},{12,4},{1,9},{9,1},{5,13},{13,5},{2,10},{10,2},... | collective-permute-start | bytes 3145736 | tf_op jit(solution)/shard_map/ppermute | solution.py:349
  6.0 1.7 %collective-permute-start.4 = (f32[8,128,256]{2,1,0:T(8,128)}, f32[8,128,256]{2,1,0:T(8,128)}, u32[]{:S(2)}, u32[]{:S(2)}) collective-permute-start(f32[8,128,256]{2,1,0:T(8,128)} %bitcast.9), channel_id=1, source_target_pairs={{1,2},{2,1},{5,6},{6,5},{9,10},{10,9},{13,14},{14,13},{17,18},{18,... | collective-permute-start | bytes 3145736 | tf_op jit(solution)/shard_map/ppermute | solution.py:347
  7.7 18.7 %collective-permute-done.refs_9_ = f32[8,128,256]{2,1,0:T(8,128)S(1)} collective-permute-done((f32[8,128,256]{2,1,0:T(8,128)}, f32[8,128,256]{2,1,0:T(8,128)S(1)}, u32[]{:S(2)}, u32[]{:S(2)}) %collective-permute-start) | collective-permute-done | bytes 1048608 | tf_op jit(solution)/shard_map/ppermute | solution.py:346
  26.4 1.5 %collective-permute-done.1.refs_4_ = f32[8,128,256]{2,1,0:T(8,128)S(1)} collective-permute-done((f32[8,128,256]{2,1,0:T(8,128)}, f32[8,128,256]{2,1,0:T(8,128)S(1)}, u32[]{:S(2)}, u32[]{:S(2)}) %collective-permute-start.1) | collective-permute-done | bytes 1048608 | tf_op jit(solution)/shard_map/ppermute | solution.py:348
  27.9 1.2 %collective-permute-done.2.refs_5_ = f32[8,128,256]{2,1,0:T(8,128)S(1)} collective-permute-done((f32[8,128,256]{2,1,0:T(8,128)}, f32[8,128,256]{2,1,0:T(8,128)S(1)}, u32[]{:S(2)}, u32[]{:S(2)}) %collective-permute-start.2) | collective-permute-done | bytes 1048608 | tf_op jit(solution)/shard_map/ppermute | solution.py:349
  29.1 1.6 %collective-permute-start.3 = (f32[8,128,256]{2,1,0:T(8,128)S(1)}, f32[8,128,256]{2,1,0:T(8,128)}, u32[]{:S(2)}, u32[]{:S(2)}) collective-permute-start(f32[8,128,256]{2,1,0:T(8,128)S(1)} %collective-permute-done.refs_9_), channel_id=1, source_target_pairs={{1,2},{2,1},{5,6},{6,5},{9,10},{10,9},{13,14},{14,13},{17,18},{18,... | collective-permute-start | bytes 3145736 | tf_op jit(solution)/shard_map/ppermute | solution.py:360
  30.7 1.3 %collective-permute-start.5 = (f32[8,128,256]{2,1,0:T(8,128)}, f32[8,128,256]{2,1,0:T(8,128)}, u32[]{:S(2)}, u32[]{:S(2)}) collective-permute-start(f32[8,128,256]{2,1,0:T(8,128)} %collective-permute-done.4.refs_11_.refs_16_), channel_id=1, source_target_pairs={{1,0},{2,3},{5,4},{6,7},{9,8},{10,11},{13,12},{14,15},{17,16},{18,... | collective-permute-start | bytes 3145736 | tf_op jit(solution)/shard_map/ppermute | solution.py:359
  32.0 1.6 %collective-permute-start.6 = (f32[2,128,256]{2,1,0:T(8,128)S(1)}, f32[2,128,256]{2,1,0:T(8,128)S(1)}, u32[]{:S(2)}, u32[]{:S(2)}) collective-permute-start(f32[2,128,256]{2,1,0:T(8,128)S(1)} %get-tuple-element.60), channel_id=1, source_target_pairs={{0,8},{8,0},{4,12},{12,4},{1,9},{9,1},{5,13},{13,5},{2,10},{10,2},... | collective-permute-start | bytes 786440 | tf_op jit(solution)/shard_map/ppermute | solution.py:355
  33.6 0.7 fusion
  34.3 0.5 collective-permute-start.7
  34.9 0.5 collective-permute-start.8
  35.4 5.9 %collective-permute-done.6.refs_6_ = f32[2,128,256]{2,1,0:T(8,128)S(1)} collective-permute-done((f32[2,128,256]{2,1,0:T(8,128)S(1)}, f32[2,128,256]{2,1,0:T(8,128)S(1)}, u32[]{:S(2)}, u32[]{:S(2)}) %collective-permute-start.6) | collective-permute-done | bytes 262176 | tf_op jit(solution)/shard_map/ppermute | solution.py:355
  41.8 0.7 collective-permute-done.7.refs_7_
  42.6 0.7 copy-done.13
  43.3 11.9 %shard_map.55 = (f32[1024,1024]{1,0:T(8,128)}, bf16[4,1024,256]{2,1,0:T(8,128)(2,1)}, bf16[4,1024,256]{2,1,0:T(8,128)(2,1)}, f32[1,1024,256]{2,1,0:T(8,128)}, f32[1,1024,256]{2,1,0:T(8,128)}) custom-call(f32[1024,1024]{1,0:T(8,128)} %refs_0_.1, s32[8,4,128]{2,1,0:T(4,128)} %bitcast.12, s32[8,1,512]{2,1,0:T(1,128)} %bitcast.20, f32[8,128,256]{2,1,0:T(8,128)} %bitcast.6, ...), custom_call_target="tpu_custom_call" | custom-call | flops 1000 | bytes 1000 | tf_op jit(solution)/shard_map/pallas_call | solution.py:309
  55.3 0.5 collective-permute-start.12
  55.8 1.5 %collective-permute-done.5.refs_10_.refs_15_ = f32[8,128,256]{2,1,0:T(8,128)} collective-permute-done((f32[8,128,256]{2,1,0:T(8,128)}, f32[8,128,256]{2,1,0:T(8,128)}, u32[]{:S(2)}, u32[]{:S(2)}) %collective-permute-start.5) | collective-permute-done | bytes 1048608 | tf_op jit(solution)/shard_map/ppermute | solution.py:359
  57.2 1.2 %slice.23.refs_5_.refs_10_ = f32[6,128,256]{2,1,0:T(8,128)S(1)} slice(f32[8,128,256]{2,1,0:T(8,128)} %collective-permute-done.3), slice={[2:8], [0:128], [0:256]} | slice | bytes 1572864 | tf_op jit(solution)/shard_map/slice | solution.py:380
  58.5 1.3 %collective-permute-start.13 = (f32[6,128,256]{2,1,0:T(8,128)S(1)}, f32[6,128,256]{2,1,0:T(8,128)S(1)}, u32[]{:S(2)}, u32[]{:S(2)}) collective-permute-start(f32[6,128,256]{2,1,0:T(8,128)S(1)} %slice.23.refs_5_.refs_10_), channel_id=1, source_target_pairs={{1,0},{2,3},{5,4},{6,7},{9,8},{10,11},{13,12},{14,15},{17,16},{18,... | collective-permute-start | bytes 2359304 | tf_op jit(solution)/shard_map/ppermute | solution.py:381
  59.8 1.0 slice.22.refs_7_.refs_11_
  60.8 1.3 %collective-permute-start.15 = (f32[2,128,256]{2,1,0:T(8,128)S(1)}, f32[2,128,256]{2,1,0:T(8,128)S(1)}, u32[]{:S(2)}, u32[]{:S(2)}) collective-permute-start(f32[2,128,256]{2,1,0:T(8,128)S(1)} %slice.22.refs_7_.refs_11_), channel_id=1, source_target_pairs={{1,0},{2,3},{5,4},{6,7},{9,8},{10,11},{13,12},{14,15},{17,16},{18,... | collective-permute-start | bytes 786440 | tf_op jit(solution)/shard_map/ppermute | solution.py:382
  62.1 17.1 %shard_map.56 = (f32[1024,1024]{1,0:T(8,128)}, bf16[4,1024,256]{2,1,0:T(8,128)(2,1)}, bf16[4,1024,256]{2,1,0:T(8,128)(2,1)}) custom-call(f32[1024,1024]{1,0:T(8,128)} %get-tuple-element.35.refs_0_, s32[8,4,128]{2,1,0:T(4,128)} %bitcast.13, s32[8,1,512]{2,1,0:T(1,128)} %bitcast.21, f32[8,128,256]{2,1,0:T(8,128)} %bitcast.7, f32[8,128,256]{2,1,0:T(8,128)} %copy-done.1, ...), custom_call_target="tpu_custom_call" | custom-call | flops 1000 | bytes 1000 | tf_op jit(solution)/shard_map/pallas_call | solution.py:309
  79.3 2.0 %collective-permute-done.13.refs_4_.refs_9_ = f32[6,128,256]{2,1,0:T(8,128)S(1)} collective-permute-done((f32[6,128,256]{2,1,0:T(8,128)S(1)}, f32[6,128,256]{2,1,0:T(8,128)S(1)}, u32[]{:S(2)}, u32[]{:S(2)}) %collective-permute-start.13) | collective-permute-done | bytes 786464 | tf_op jit(solution)/shard_map/ppermute | solution.py:381
  81.3 0.9 copy-done.4
  82.1 7.2 %shard_map.57 = (f32[512,1024]{1,0:T(8,128)}, f32[512,1024]{1,0:T(8,128)}) custom-call(f32[1024,1024]{1,0:T(8,128)} %get-tuple-element.47.refs_0_, s32[8,4,128]{2,1,0:T(4,128)} %bitcast.15, bf16[4,1024,256]{2,1,0:T(8,128)(2,1)} %get-tuple-element.41.refs_13_.refs_2_, bf16[4,1024,256]{2,1,0:T(8,128)(2,1)} %get-tuple-element.42.refs_14_.refs_3_, ...), custom_call_target="tpu_custom_call" | custom-call | flops 1000 | bytes 1000 | tf_op jit(solution)/shard_map/pallas_call | solution.py:309
  89.4 0.5 collective-permute-start.14
  90.4 6.1 %collective-permute-done.17.refs_12_.refs_16_ = s32[8,4,128]{2,1,0:T(4,128)S(1)} collective-permute-done((s32[8,4,128]{2,1,0:T(4,128)S(1)}, s32[8,4,128]{2,1,0:T(4,128)S(1)}, u32[]{:S(2)}, u32[]{:S(2)}) %collective-permute-start.17) | collective-permute-done | bytes 16416 | tf_op jit(solution)/shard_map/ppermute | solution.py:363
  96.6 0.7 collective-permute-done.14.refs_2_
  97.3 0.7 copy-done.6
  98.0 7.6 %shard_map.58 = f32[1024,1024]{1,0:T(8,128)} custom-call(f32[512,1024]{1,0:T(8,128)} %get-tuple-element.50.refs_0_, f32[512,1024]{1,0:T(8,128)} %get-tuple-element.52.refs_1_, f32[512,1024]{1,0:T(8,128)} %collective-permute-done.14.refs_2_, f32[512,1024]{1,0:T(8,128)} %copy-done.6, s32[8,4,128]{2,1,0:T(4,128)} %bitcast.17, ...), custom_call_target="tpu_custom_call" | custom-call | flops 1000 | bytes 1000 | tf_op jit(solution)/shard_map/pallas_call | solution.py:309
  (44 shorter events, 1.3 us)
Async XLA Ops:
  0.0 26.4 %collective-permute-start = (f32[8,128,256]{2,1,0:T(8,128)}, f32[8,128,256]{2,1,0:T(8,128)S(1)}, u32[]{:S(2)}, u32[]{:S(2)}) collective-permute-start(f32[8,128,256]{2,1,0:T(8,128)} %bitcast.8), channel_id=1, source_target_pairs={{0,1},{1,0},{2,3},{3,2},{4,5},{5,4},{6,7},{7,6},{8,9},{9,8},{10,11... | collective-permute-start | bytes 3145736 | tf_op jit(solution)/shard_map/ppermute | solution.py:346
  3.0 24.8 %collective-permute-start.1 = (f32[8,128,256]{2,1,0:T(8,128)}, f32[8,128,256]{2,1,0:T(8,128)S(1)}, u32[]{:S(2)}, u32[]{:S(2)}) collective-permute-start(f32[8,128,256]{2,1,0:T(8,128)} %bitcast.4), channel_id=1, source_target_pairs={{0,4},{4,0},{8,12},{12,8},{1,5},{5,1},{9,13},{13,9},{2,6},{6,2},{1... | collective-permute-start | bytes 3145736 | tf_op jit(solution)/shard_map/ppermute | solution.py:348
  4.5 24.5 %collective-permute-start.2 = (f32[8,128,256]{2,1,0:T(8,128)}, f32[8,128,256]{2,1,0:T(8,128)S(1)}, u32[]{:S(2)}, u32[]{:S(2)}) collective-permute-start(f32[8,128,256]{2,1,0:T(8,128)} %bitcast.5), channel_id=1, source_target_pairs={{0,8},{8,0},{4,12},{12,4},{1,9},{9,1},{5,13},{13,5},{2,10},{10,2},... | collective-permute-start | bytes 3145736 | tf_op jit(solution)/shard_map/ppermute | solution.py:349
  6.0 24.7 %collective-permute-start.4 = (f32[8,128,256]{2,1,0:T(8,128)}, f32[8,128,256]{2,1,0:T(8,128)}, u32[]{:S(2)}, u32[]{:S(2)}) collective-permute-start(f32[8,128,256]{2,1,0:T(8,128)} %bitcast.9), channel_id=1, source_target_pairs={{1,2},{2,1},{5,6},{6,5},{9,10},{10,9},{13,14},{14,13},{17,18},{18,... | collective-permute-start | bytes 3145736 | tf_op jit(solution)/shard_map/ppermute | solution.py:347
  26.4 16.2 %copy-start.3 = (f32[8,128,256]{2,1,0:T(8,128)}, f32[8,128,256]{2,1,0:T(8,128)S(1)}, u32[]{:S(2)}) copy-start(f32[8,128,256]{2,1,0:T(8,128)S(1)} %collective-permute-done.refs_9_) | copy-start | bytes 3145732
  27.9 14.7 %copy-start.1 = (f32[8,128,256]{2,1,0:T(8,128)}, f32[8,128,256]{2,1,0:T(8,128)S(1)}, u32[]{:S(2)}) copy-start(f32[8,128,256]{2,1,0:T(8,128)S(1)} %collective-permute-done.1.refs_4_) | copy-start | bytes 3145732
  29.1 13.5 %copy-start.2 = (f32[8,128,256]{2,1,0:T(8,128)}, f32[8,128,256]{2,1,0:T(8,128)S(1)}, u32[]{:S(2)}) copy-start(f32[8,128,256]{2,1,0:T(8,128)S(1)} %collective-permute-done.2.refs_5_) | copy-start | bytes 3145732
  29.1 26.7 %collective-permute-start.3 = (f32[8,128,256]{2,1,0:T(8,128)S(1)}, f32[8,128,256]{2,1,0:T(8,128)}, u32[]{:S(2)}, u32[]{:S(2)}) collective-permute-start(f32[8,128,256]{2,1,0:T(8,128)S(1)} %collective-permute-done.refs_9_), channel_id=1, source_target_pairs={{1,2},{2,1},{5,6},{6,5},{9,10},{10,9},{13,14},{14,13},{17,18},{18,... | collective-permute-start | bytes 3145736 | tf_op jit(solution)/shard_map/ppermute | solution.py:360
  30.7 26.5 %collective-permute-start.5 = (f32[8,128,256]{2,1,0:T(8,128)}, f32[8,128,256]{2,1,0:T(8,128)}, u32[]{:S(2)}, u32[]{:S(2)}) collective-permute-start(f32[8,128,256]{2,1,0:T(8,128)} %collective-permute-done.4.refs_11_.refs_16_), channel_id=1, source_target_pairs={{1,0},{2,3},{5,4},{6,7},{9,8},{10,11},{13,12},{14,15},{17,16},{18,... | collective-permute-start | bytes 3145736 | tf_op jit(solution)/shard_map/ppermute | solution.py:359
  32.0 9.3 %collective-permute-start.6 = (f32[2,128,256]{2,1,0:T(8,128)S(1)}, f32[2,128,256]{2,1,0:T(8,128)S(1)}, u32[]{:S(2)}, u32[]{:S(2)}) collective-permute-start(f32[2,128,256]{2,1,0:T(8,128)S(1)} %get-tuple-element.60), channel_id=1, source_target_pairs={{0,8},{8,0},{4,12},{12,4},{1,9},{9,1},{5,13},{13,5},{2,10},{10,2},... | collective-permute-start | bytes 786440 | tf_op jit(solution)/shard_map/ppermute | solution.py:355
  34.3 8.2 %collective-permute-start.7 = (f32[2,128,256]{2,1,0:T(8,128)S(1)}, f32[2,128,256]{2,1,0:T(8,128)S(1)}, u32[]{:S(2)}, u32[]{:S(2)}) collective-permute-start(f32[2,128,256]{2,1,0:T(8,128)S(1)} %get-tuple-element.58), channel_id=1, source_target_pairs={{0,4},{4,0},{8,12},{12,8},{1,5},{5,1},{9,13},{13,9},{2,6},{6,2},{1... | collective-permute-start | bytes 786440 | tf_op jit(solution)/shard_map/ppermute | solution.py:356
  34.9 20.3 %collective-permute-start.8 = (f32[2,128,256]{2,1,0:T(8,128)S(1)}, f32[2,128,256]{2,1,0:T(8,128)}, u32[]{:S(2)}, u32[]{:S(2)}) collective-permute-start(f32[2,128,256]{2,1,0:T(8,128)S(1)} %get-tuple-element.59), channel_id=1, source_target_pairs={{0,8},{8,0},{4,12},{12,4},{1,9},{9,1},{5,13},{13,5},{2,10},{10,2},... | collective-permute-start | bytes 786440 | tf_op jit(solution)/shard_map/ppermute | solution.py:355
  41.3 1.2 %copy-start.12 = (f32[2,128,256]{2,1,0:T(8,128)}, f32[2,128,256]{2,1,0:T(8,128)S(1)}, u32[]{:S(2)}) copy-start(f32[2,128,256]{2,1,0:T(8,128)S(1)} %collective-permute-done.6.refs_6_) | copy-start | bytes 786436
  41.3 13.8 %collective-permute-start.9 = (f32[2,128,256]{2,1,0:T(8,128)}, f32[2,128,256]{2,1,0:T(8,128)}, u32[]{:S(2)}, u32[]{:S(2)}) collective-permute-start(f32[2,128,256]{2,1,0:T(8,128)} %get-tuple-element.57), channel_id=1, source_target_pairs={{0,4},{4,0},{8,12},{12,8},{1,5},{5,1},{9,13},{13,9},{2,6},{6,2},{1... | collective-permute-start | bytes 786440 | tf_op jit(solution)/shard_map/ppermute | solution.py:356
  55.2 24.1 %collective-permute-start.11 = (f32[1,1024,256]{2,1,0:T(8,128)}, f32[1,1024,256]{2,1,0:T(8,128)S(1)}, u32[]{:S(2)}, u32[]{:S(2)}) collective-permute-start(f32[1,1024,256]{2,1,0:T(8,128)} %get-tuple-element.45.refs_5_), channel_id=1, source_target_pairs={{0,16},{16,0},{1,17},{17,1},{2,18},{18,2},{3,19},{19,3},{4,20},{20... | collective-permute-start | bytes 3145736 | tf_op jit(solution)/shard_map/ppermute | solution.py:385
  55.3 24.0 %collective-permute-start.12 = (f32[1,1024,256]{2,1,0:T(8,128)}, f32[1,1024,256]{2,1,0:T(8,128)}, u32[]{:S(2)}, u32[]{:S(2)}) collective-permute-start(f32[1,1024,256]{2,1,0:T(8,128)} %get-tuple-element.46.refs_9_), channel_id=1, source_target_pairs={{0,16},{16,0},{1,17},{17,1},{2,18},{18,2},{3,19},{19,3},{4,20},{20... | collective-permute-start | bytes 3145736 | tf_op jit(solution)/shard_map/ppermute | solution.py:385
  58.4 20.8 %copy-start = (f32[6,128,256]{2,1,0:T(8,128)}, f32[6,128,256]{2,1,0:T(8,128)S(1)}, u32[]{:S(2)}) copy-start(f32[6,128,256]{2,1,0:T(8,128)S(1)} %slice.23.refs_5_.refs_10_) | copy-start | bytes 2359300
  58.5 22.8 %collective-permute-start.13 = (f32[6,128,256]{2,1,0:T(8,128)S(1)}, f32[6,128,256]{2,1,0:T(8,128)S(1)}, u32[]{:S(2)}, u32[]{:S(2)}) collective-permute-start(f32[6,128,256]{2,1,0:T(8,128)S(1)} %slice.23.refs_5_.refs_10_), channel_id=1, source_target_pairs={{1,0},{2,3},{5,4},{6,7},{9,8},{10,11},{13,12},{14,15},{17,16},{18,... | collective-permute-start | bytes 2359304 | tf_op jit(solution)/shard_map/ppermute | solution.py:381
  60.7 18.5 %copy-start.5 = (f32[2,128,256]{2,1,0:T(8,128)}, f32[2,128,256]{2,1,0:T(8,128)S(1)}, u32[]{:S(2)}) copy-start(f32[2,128,256]{2,1,0:T(8,128)S(1)} %slice.22.refs_7_.refs_11_) | copy-start | bytes 786436
  60.7 18.5 %collective-permute-start.10 = (f32[2,128,256]{2,1,0:T(8,128)S(1)}, f32[2,128,256]{2,1,0:T(8,128)S(1)}, u32[]{:S(2)}, u32[]{:S(2)}) collective-permute-start(f32[2,128,256]{2,1,0:T(8,128)S(1)} %slice.22.refs_7_.refs_11_), channel_id=1, source_target_pairs={{0,16},{16,0},{1,17},{17,1},{2,18},{18,2},{3,19},{19,3},{4,20},{20... | collective-permute-start | bytes 786440 | tf_op jit(solution)/shard_map/ppermute | solution.py:383
  60.8 28.5 %collective-permute-start.15 = (f32[2,128,256]{2,1,0:T(8,128)S(1)}, f32[2,128,256]{2,1,0:T(8,128)S(1)}, u32[]{:S(2)}, u32[]{:S(2)}) collective-permute-start(f32[2,128,256]{2,1,0:T(8,128)S(1)} %slice.22.refs_7_.refs_11_), channel_id=1, source_target_pairs={{1,0},{2,3},{5,4},{6,7},{9,8},{10,11},{13,12},{14,15},{17,16},{18,... | collective-permute-start | bytes 786440 | tf_op jit(solution)/shard_map/ppermute | solution.py:382
  79.2 10.1 %copy-start.10 = (f32[1,1024,256]{2,1,0:T(8,128)}, f32[1,1024,256]{2,1,0:T(8,128)S(1)}, u32[]{:S(2)}) copy-start(f32[1,1024,256]{2,1,0:T(8,128)S(1)} %collective-permute-done.11.refs_13_) | copy-start | bytes 3145732
  79.3 10.1 %copy-start.7 = (f32[2,128,256]{2,1,0:T(8,128)}, f32[2,128,256]{2,1,0:T(8,128)S(1)}, u32[]{:S(2)}) copy-start(f32[2,128,256]{2,1,0:T(8,128)S(1)} %collective-permute-done.10.refs_15_.refs_19_) | copy-start | bytes 786436
  81.2 0.9 copy-start.4
  82.1 7.9 %copy-start.11 = (s32[1,8,1,512]{3,2,1,0:T(1,128)S(1)}, s32[1,8,1,512]{3,2,1,0:T(1,128)}, u32[]{:S(2)}) copy-start(s32[1,8,1,512]{3,2,1,0:T(1,128)} %param.7) | copy-start | bytes 49156
  89.3 8.0 %copy-start.8 = (f32[2,128,256]{2,1,0:T(8,128)}, f32[2,128,256]{2,1,0:T(8,128)S(1)}, u32[]{:S(2)}) copy-start(f32[2,128,256]{2,1,0:T(8,128)S(1)} %collective-permute-done.15.refs_6_.refs_10_) | copy-start | bytes 786436
  89.4 7.2 %collective-permute-start.16 = (f32[512,1024]{1,0:T(8,128)}, f32[512,1024]{1,0:T(8,128)S(1)}, u32[]{:S(2)}, u32[]{:S(2)}) collective-permute-start(f32[512,1024]{1,0:T(8,128)} %get-tuple-element.52.refs_1_), channel_id=1, source_target_pairs={{0,16},{16,0},{1,17},{17,1},{2,18},{18,2},{3,19},{19,3},{4,20},{20... | collective-permute-start | bytes 6291464 | tf_op jit(solution)/shard_map/ppermute | solution.py:426
  89.4 7.9 %collective-permute-start.14 = (f32[512,1024]{1,0:T(8,128)}, f32[512,1024]{1,0:T(8,128)}, u32[]{:S(2)}, u32[]{:S(2)}) collective-permute-start(f32[512,1024]{1,0:T(8,128)} %get-tuple-element.50.refs_0_), channel_id=1, source_target_pairs={{0,16},{16,0},{1,17},{17,1},{2,18},{18,2},{3,19},{19,3},{4,20},{20... | collective-permute-start | bytes 6291464 | tf_op jit(solution)/shard_map/ppermute | solution.py:423
  89.9 6.7 %collective-permute-start.18 = (f32[2,128,256]{2,1,0:T(8,128)S(1)}, f32[2,128,256]{2,1,0:T(8,128)S(1)}, u32[]{:S(2)}, u32[]{:S(2)}) collective-permute-start(f32[2,128,256]{2,1,0:T(8,128)S(1)} %collective-permute-done.15.refs_6_.refs_10_), channel_id=1, source_target_pairs={{0,16},{16,0},{1,17},{17,1},{2,18},{18,2},{3,19},{19,3},{4,20},{20... | collective-permute-start | bytes 786440 | tf_op jit(solution)/shard_map/ppermute | solution.py:425
  90.0 6.6 %collective-permute-start.17 = (s32[8,4,128]{2,1,0:T(4,128)S(1)}, s32[8,4,128]{2,1,0:T(4,128)S(1)}, u32[]{:S(2)}, u32[]{:S(2)}) collective-permute-start(s32[8,4,128]{2,1,0:T(4,128)S(1)} %bitcast.19), channel_id=1, source_target_pairs={{0,16},{16,0},{1,17},{17,1},{2,18},{18,2},{3,19},{19,3},{4,20},{20... | collective-permute-start | bytes 49160 | tf_op jit(solution)/shard_map/ppermute | solution.py:363
  96.6 0.7 copy-start.14
  96.6 1.4 %copy-start.6 = (f32[512,1024]{1,0:T(8,128)}, f32[512,1024]{1,0:T(8,128)S(1)}, u32[]{:S(2)}) copy-start(f32[512,1024]{1,0:T(8,128)S(1)} %collective-permute-done.16.refs_3_) | copy-start | bytes 6291460
  (2 other events, 1.4 us)

commit v5 on v4

--- a/solution.py
+++ b/solution.py
@@ -9,7 +9,7 @@
 
 F32 = jnp.float32
 BF16 = jnp.bfloat16
-VMEM_ALL = 60 * 1024 * 1024
+VMEM_ALL = 127 * 512 * 1024
 
 
 def spread_dense(row_panel, row_map, col_dense, row_count):
@@ -376,8 +376,8 @@
 
     mine, *dense1 = near([front_matrix], 0, first, by_xy1, emit_sums=late, one_layer=True)
     dense1, sums = dense1[:2], dense1[2:]
-    far_b, mid_a, mine = together((far_b, mid_a, mine))
     far_b2, far_b1 = far_b[:late], far_b[late:]
+    far_b1, far_b2, mid_a, mine = together((far_b1, far_b2, mid_a, mine))
     far_a1 = lax.ppermute(far_b1, "col", OUTWARD)
     far_a2 = lax.ppermute(far_b2, "col", OUTWARD)
     far_b2_other = lax.ppermute(far_b2, "gz", swap)

time: 106 us -> 107 us (level)
  waiting for transfers between devices: 38.3 us -> 39.8 us
    ppermute x1, waiting for transfers between devices: 6.15 us -> 3.2 us  [four_by_four(): row_map_other = lax.ppermute(row_map, 'gz', swap)]
    ppermute x1, waiting for transfers between devices: 1.96 us -> 4.75 us  [four_by_four(): far_a1 = lax.ppermute(far_b1, 'col', OUTWARD)]
    unnamed x30 -> x14, local copies, waits for them, and re-layouts: 2.28 us -> 0.03 us
    ppermute x1, waiting for transfers between devices: 0.7 us -> 2.75 us  [four_by_four(): other_top = lax.ppermute(top, 'gz', swap)]
    ppermute x1, waiting for transfers between devices: 1.47 us -> 0.01 us  [four_by_four(): mid_a = lax.ppermute(mid_b, 'col', OUTWARD)]
  transfers between devices with their start and end apart: 19 -> 19, of which waited for: 9 -> 9; matrix products, arithmetic and copies ran while one was open for 3% -> 4% of each run, Pallas kernels for 34% -> 34%
where the time goes in v5:
time: 107 us; the launch traced here: 106 us
  Pallas kernels  43.7 us (41%)
  waiting for transfers between devices  39.8 us (37%)
  starting transfers between devices  18 us (17%)
  local copies, waits for them, and re-layouts  4.6 us (4%)
    pallas_call x4, Pallas kernels, stage(): pl.pallas_call(functools.partial(stage_kernel, plan), in_specs=[pl.BlockS...  43.7 us
    ppermute x1, waiting for transfers between devices, four_by_four(): pair = lax.ppermute(l_own, 'col', ENDS)  18.8 us
    ppermute x2, waiting for transfers between devices, diagonal(): lax.ppermute(by_x[start:cut], 'row', SWAP_Y)  5.93 us
    ppermute x1, waiting for transfers between devices, four_by_four(): far_a1 = lax.ppermute(far_b1, 'col', OUTWARD)  4.75 us
    ppermute x1, waiting for transfers between devices, four_by_four(): row_map_other = lax.ppermute(row_map, 'gz', swap)  3.2 us
    slice x2, local copies, waits for them, and re-layouts, four_by_four(): far_b2, far_b1 = (far_b[:late], far_b[late:])  3.08 us
    ppermute x1, starting transfers between devices, four_by_four(): pair = lax.ppermute(l_own, 'col', ENDS)  3.02 us
    ppermute x1, waiting for transfers between devices, four_by_four(): other_top = lax.ppermute(top, 'gz', swap)  2.75 us
  transfers between devices with their start and end apart: 19, of which 9 were waited for; matrix products, arithmetic and copies ran while one was open for 4% of the time, Pallas kernels for 34%

profile of v5, /device:TPU:0, one launch (start us, length us, event | category | flops | bytes accessed | tf_op | source)
XLA Modules:
  0.0 106.3 jit_solution(1493887028730554749)
XLA Ops:
  0.0 3.0 %collective-permute-start = (f32[8,128,256]{2,1,0:T(8,128)}, f32[8,128,256]{2,1,0:T(8,128)}, u32[]{:S(2)}, u32[]{:S(2)}) collective-permute-start(f32[8,128,256]{2,1,0:T(8,128)} %bitcast.8), channel_id=1, source_target_pairs={{0,1},{1,0},{2,3},{3,2},{4,5},{5,4},{6,7},{7,6},{8,9},{9,8},{10,11... | collective-permute-start | bytes 3145736 | tf_op jit(solution)/shard_map/ppermute | solution.py:346
  3.0 1.5 %collective-permute-start.1 = (f32[8,128,256]{2,1,0:T(8,128)}, f32[8,128,256]{2,1,0:T(8,128)S(1)}, u32[]{:S(2)}, u32[]{:S(2)}) collective-permute-start(f32[8,128,256]{2,1,0:T(8,128)} %bitcast.4), channel_id=1, source_target_pairs={{0,4},{4,0},{8,12},{12,8},{1,5},{5,1},{9,13},{13,9},{2,6},{6,2},{1... | collective-permute-start | bytes 3145736 | tf_op jit(solution)/shard_map/ppermute | solution.py:348
  4.5 1.5 %collective-permute-start.2 = (f32[8,128,256]{2,1,0:T(8,128)}, f32[8,128,256]{2,1,0:T(8,128)S(1)}, u32[]{:S(2)}, u32[]{:S(2)}) collective-permute-start(f32[8,128,256]{2,1,0:T(8,128)} %bitcast.5), channel_id=1, source_target_pairs={{0,8},{8,0},{4,12},{12,4},{1,9},{9,1},{5,13},{13,5},{2,10},{10,2},... | collective-permute-start | bytes 3145736 | tf_op jit(solution)/shard_map/ppermute | solution.py:349
  6.0 1.7 %collective-permute-start.4 = (f32[8,128,256]{2,1,0:T(8,128)}, f32[8,128,256]{2,1,0:T(8,128)}, u32[]{:S(2)}, u32[]{:S(2)}) collective-permute-start(f32[8,128,256]{2,1,0:T(8,128)} %bitcast.9), channel_id=1, source_target_pairs={{1,2},{2,1},{5,6},{6,5},{9,10},{10,9},{13,14},{14,13},{17,18},{18,... | collective-permute-start | bytes 3145736 | tf_op jit(solution)/shard_map/ppermute | solution.py:347
  7.7 18.8 %collective-permute-done.refs_9_ = f32[8,128,256]{2,1,0:T(8,128)} collective-permute-done((f32[8,128,256]{2,1,0:T(8,128)}, f32[8,128,256]{2,1,0:T(8,128)}, u32[]{:S(2)}, u32[]{:S(2)}) %collective-permute-start) | collective-permute-done | bytes 1048608 | tf_op jit(solution)/shard_map/ppermute | solution.py:346
  26.5 1.4 %collective-permute-done.1.refs_4_ = f32[8,128,256]{2,1,0:T(8,128)S(1)} collective-permute-done((f32[8,128,256]{2,1,0:T(8,128)}, f32[8,128,256]{2,1,0:T(8,128)S(1)}, u32[]{:S(2)}, u32[]{:S(2)}) %collective-permute-start.1) | collective-permute-done | bytes 1048608 | tf_op jit(solution)/shard_map/ppermute | solution.py:348
  27.9 1.2 %collective-permute-done.2.refs_5_ = f32[8,128,256]{2,1,0:T(8,128)S(1)} collective-permute-done((f32[8,128,256]{2,1,0:T(8,128)}, f32[8,128,256]{2,1,0:T(8,128)S(1)}, u32[]{:S(2)}, u32[]{:S(2)}) %collective-permute-start.2) | collective-permute-done | bytes 1048608 | tf_op jit(solution)/shard_map/ppermute | solution.py:349
  29.1 1.6 %collective-permute-start.3 = (f32[8,128,256]{2,1,0:T(8,128)}, f32[8,128,256]{2,1,0:T(8,128)}, u32[]{:S(2)}, u32[]{:S(2)}) collective-permute-start(f32[8,128,256]{2,1,0:T(8,128)} %collective-permute-done.refs_9_), channel_id=1, source_target_pairs={{1,2},{2,1},{5,6},{6,5},{9,10},{10,9},{13,14},{14,13},{17,18},{18,... | collective-permute-start | bytes 3145736 | tf_op jit(solution)/shard_map/ppermute | solution.py:360
  30.7 1.3 %collective-permute-start.5 = (f32[8,128,256]{2,1,0:T(8,128)}, f32[8,128,256]{2,1,0:T(8,128)}, u32[]{:S(2)}, u32[]{:S(2)}) collective-permute-start(f32[8,128,256]{2,1,0:T(8,128)} %collective-permute-done.4.refs_11_.refs_16_), channel_id=1, source_target_pairs={{1,0},{2,3},{5,4},{6,7},{9,8},{10,11},{13,12},{14,15},{17,16},{18,... | collective-permute-start | bytes 3145736 | tf_op jit(solution)/shard_map/ppermute | solution.py:359
  32.0 0.8 fusion.1
  32.8 1.5 %collective-permute-start.6 = (f32[2,128,256]{2,1,0:T(8,128)S(1)}, f32[2,128,256]{2,1,0:T(8,128)S(1)}, u32[]{:S(2)}, u32[]{:S(2)}) collective-permute-start(f32[2,128,256]{2,1,0:T(8,128)S(1)} %get-tuple-element.62), channel_id=1, source_target_pairs={{0,8},{8,0},{4,12},{12,4},{1,9},{9,1},{5,13},{13,5},{2,10},{10,2},... | collective-permute-start | bytes 786440 | tf_op jit(solution)/shard_map/ppermute | solution.py:355
  34.3 0.7 fusion
  35.0 0.5 collective-permute-start.7
  35.6 0.5 collective-permute-start.8
  36.1 5.9 %collective-permute-done.6.refs_6_ = f32[2,128,256]{2,1,0:T(8,128)S(1)} collective-permute-done((f32[2,128,256]{2,1,0:T(8,128)S(1)}, f32[2,128,256]{2,1,0:T(8,128)S(1)}, u32[]{:S(2)}, u32[]{:S(2)}) %collective-permute-start.6) | collective-permute-done | bytes 262176 | tf_op jit(solution)/shard_map/ppermute | solution.py:355
  42.0 0.5 collective-permute-start.9
  42.5 0.9 collective-permute-done.7.refs_7_
  43.4 11.9 %shard_map.55 = (f32[1024,1024]{1,0:T(8,128)}, bf16[4,1024,256]{2,1,0:T(8,128)(2,1)}, bf16[4,1024,256]{2,1,0:T(8,128)(2,1)}, f32[1,1024,256]{2,1,0:T(8,128)}, f32[1,1024,256]{2,1,0:T(8,128)}) custom-call(f32[1024,1024]{1,0:T(8,128)} %refs_0_.1, s32[8,4,128]{2,1,0:T(4,128)} %bitcast.12, s32[8,1,512]{2,1,0:T(1,128)} %bitcast.20, f32[8,128,256]{2,1,0:T(8,128)} %bitcast.6, ...), custom_call_target="tpu_custom_call" | custom-call | flops 1000 | bytes 1000 | tf_op jit(solution)/shard_map/pallas_call | solution.py:309
  55.4 0.5 collective-permute-start.12
  55.9 2.1 %slice.24.refs_5_.refs_10_ = f32[6,128,256]{2,1,0:T(8,128)} slice(f32[8,128,256]{2,1,0:T(8,128)} %collective-permute-done.3), slice={[2:8], [0:128], [0:256]} | slice | bytes 1572864 | tf_op jit(solution)/shard_map/slice | solution.py:379
  58.0 1.0 slice.25.refs_7_.refs_11_
  59.0 1.3 %collective-permute-start.13 = (f32[6,128,256]{2,1,0:T(8,128)}, f32[6,128,256]{2,1,0:T(8,128)}, u32[]{:S(2)}, u32[]{:S(2)}) collective-permute-start(f32[6,128,256]{2,1,0:T(8,128)} %slice.24.refs_5_.refs_10_), channel_id=1, source_target_pairs={{1,0},{2,3},{5,4},{6,7},{9,8},{10,11},{13,12},{14,15},{17,16},{18,... | collective-permute-start | bytes 2359304 | tf_op jit(solution)/shard_map/ppermute | solution.py:381
  60.4 1.3 %collective-permute-start.15 = (f32[2,128,256]{2,1,0:T(8,128)S(1)}, f32[2,128,256]{2,1,0:T(8,128)}, u32[]{:S(2)}, u32[]{:S(2)}) collective-permute-start(f32[2,128,256]{2,1,0:T(8,128)S(1)} %slice.25.refs_7_.refs_11_), channel_id=1, source_target_pairs={{1,0},{2,3},{5,4},{6,7},{9,8},{10,11},{13,12},{14,15},{17,16},{18,... | collective-permute-start | bytes 786440 | tf_op jit(solution)/shard_map/ppermute | solution.py:382
  61.7 17.1 %shard_map.56 = (f32[1024,1024]{1,0:T(8,128)}, bf16[4,1024,256]{2,1,0:T(8,128)(2,1)}, bf16[4,1024,256]{2,1,0:T(8,128)(2,1)}) custom-call(f32[1024,1024]{1,0:T(8,128)} %get-tuple-element.36.refs_0_, s32[8,4,128]{2,1,0:T(4,128)} %bitcast.13, s32[8,1,512]{2,1,0:T(1,128)} %bitcast.21, f32[8,128,256]{2,1,0:T(8,128)} %bitcast.7, f32[8,128,256]{2,1,0:T(8,128)} %copy-done, ...), custom_call_target="tpu_custom_call" | custom-call | flops 1000 | bytes 1000 | tf_op jit(solution)/shard_map/pallas_call | solution.py:309
  78.8 4.7 %collective-permute-done.13.refs_4_.refs_9_ = f32[6,128,256]{2,1,0:T(8,128)} collective-permute-done((f32[6,128,256]{2,1,0:T(8,128)}, f32[6,128,256]{2,1,0:T(8,128)}, u32[]{:S(2)}, u32[]{:S(2)}) %collective-permute-start.13) | collective-permute-done | bytes 786464 | tf_op jit(solution)/shard_map/ppermute | solution.py:381
  83.6 7.2 %shard_map.57 = (f32[512,1024]{1,0:T(8,128)}, f32[512,1024]{1,0:T(8,128)}) custom-call(f32[1024,1024]{1,0:T(8,128)} %get-tuple-element.48.refs_0_, s32[8,4,128]{2,1,0:T(4,128)} %bitcast.15, bf16[4,1024,256]{2,1,0:T(8,128)(2,1)} %get-tuple-element.42.refs_13_.refs_2_, bf16[4,1024,256]{2,1,0:T(8,128)(2,1)} %get-tuple-element.43.refs_14_.refs_3_, ...), custom_call_target="tpu_custom_call" | custom-call | flops 1000 | bytes 1000 | tf_op jit(solution)/shard_map/pallas_call | solution.py:309
  90.9 0.5 collective-permute-start.14
  91.4 0.4 collective-permute-start.17
  91.9 3.2 %collective-permute-done.17.refs_12_.refs_16_ = s32[8,4,128]{2,1,0:T(4,128)S(1)} collective-permute-done((s32[8,4,128]{2,1,0:T(4,128)S(1)}, s32[8,4,128]{2,1,0:T(4,128)S(1)}, u32[]{:S(2)}, u32[]{:S(2)}) %collective-permute-start.17) | collective-permute-done | bytes 16416 | tf_op jit(solution)/shard_map/ppermute | solution.py:363
  95.1 0.9 collective-permute-done.18.refs_14_.refs_18_
  96.0 2.8 %collective-permute-done.14.refs_2_ = f32[512,1024]{1,0:T(8,128)} collective-permute-done((f32[512,1024]{1,0:T(8,128)}, f32[512,1024]{1,0:T(8,128)}, u32[]{:S(2)}, u32[]{:S(2)}) %collective-permute-start.14) | collective-permute-done | bytes 2097184 | tf_op jit(solution)/shard_map/ppermute | solution.py:423
  98.7 7.6 %shard_map.58 = f32[1024,1024]{1,0:T(8,128)} custom-call(f32[512,1024]{1,0:T(8,128)} %get-tuple-element.52.refs_0_, f32[512,1024]{1,0:T(8,128)} %get-tuple-element.54.refs_1_, f32[512,1024]{1,0:T(8,128)} %collective-permute-done.14.refs_2_, f32[512,1024]{1,0:T(8,128)} %collective-permute-done.16.refs_3_, s32[8,4,128]{2,1,0:T(4,128)} %bitcast.17, ...), custom_call_target="tpu_custom_call" | custom-call | flops 1000 | bytes 1000 | tf_op jit(solution)/shard_map/pallas_call | solution.py:309
  (28 shorter events, 0.4 us)
Async XLA Ops:
  0.0 26.5 %collective-permute-start = (f32[8,128,256]{2,1,0:T(8,128)}, f32[8,128,256]{2,1,0:T(8,128)}, u32[]{:S(2)}, u32[]{:S(2)}) collective-permute-start(f32[8,128,256]{2,1,0:T(8,128)} %bitcast.8), channel_id=1, source_target_pairs={{0,1},{1,0},{2,3},{3,2},{4,5},{5,4},{6,7},{7,6},{8,9},{9,8},{10,11... | collective-permute-start | bytes 3145736 | tf_op jit(solution)/shard_map/ppermute | solution.py:346
  3.0 24.8 %collective-permute-start.1 = (f32[8,128,256]{2,1,0:T(8,128)}, f32[8,128,256]{2,1,0:T(8,128)S(1)}, u32[]{:S(2)}, u32[]{:S(2)}) collective-permute-start(f32[8,128,256]{2,1,0:T(8,128)} %bitcast.4), channel_id=1, source_target_pairs={{0,4},{4,0},{8,12},{12,8},{1,5},{5,1},{9,13},{13,9},{2,6},{6,2},{1... | collective-permute-start | bytes 3145736 | tf_op jit(solution)/shard_map/ppermute | solution.py:348
  4.5 24.5 %collective-permute-start.2 = (f32[8,128,256]{2,1,0:T(8,128)}, f32[8,128,256]{2,1,0:T(8,128)S(1)}, u32[]{:S(2)}, u32[]{:S(2)}) collective-permute-start(f32[8,128,256]{2,1,0:T(8,128)} %bitcast.5), channel_id=1, source_target_pairs={{0,8},{8,0},{4,12},{12,4},{1,9},{9,1},{5,13},{13,5},{2,10},{10,2},... | collective-permute-start | bytes 3145736 | tf_op jit(solution)/shard_map/ppermute | solution.py:349
  6.0 24.7 %collective-permute-start.4 = (f32[8,128,256]{2,1,0:T(8,128)}, f32[8,128,256]{2,1,0:T(8,128)}, u32[]{:S(2)}, u32[]{:S(2)}) collective-permute-start(f32[8,128,256]{2,1,0:T(8,128)} %bitcast.9), channel_id=1, source_target_pairs={{1,2},{2,1},{5,6},{6,5},{9,10},{10,9},{13,14},{14,13},{17,18},{18,... | collective-permute-start | bytes 3145736 | tf_op jit(solution)/shard_map/ppermute | solution.py:347
  27.9 4.2 %copy-start = (f32[8,128,256]{2,1,0:T(8,128)}, f32[8,128,256]{2,1,0:T(8,128)S(1)}, u32[]{:S(2)}) copy-start(f32[8,128,256]{2,1,0:T(8,128)S(1)} %collective-permute-done.1.refs_4_) | copy-start | bytes 3145732
  29.1 5.2 %copy-start.1 = (f32[8,128,256]{2,1,0:T(8,128)}, f32[8,128,256]{2,1,0:T(8,128)S(1)}, u32[]{:S(2)}) copy-start(f32[8,128,256]{2,1,0:T(8,128)S(1)} %collective-permute-done.2.refs_5_) | copy-start | bytes 3145732
  29.1 26.8 %collective-permute-start.3 = (f32[8,128,256]{2,1,0:T(8,128)}, f32[8,128,256]{2,1,0:T(8,128)}, u32[]{:S(2)}, u32[]{:S(2)}) collective-permute-start(f32[8,128,256]{2,1,0:T(8,128)} %collective-permute-done.refs_9_), channel_id=1, source_target_pairs={{1,2},{2,1},{5,6},{6,5},{9,10},{10,9},{13,14},{14,13},{17,18},{18,... | collective-permute-start | bytes 3145736 | tf_op jit(solution)/shard_map/ppermute | solution.py:360
  30.7 28.2 %collective-permute-start.5 = (f32[8,128,256]{2,1,0:T(8,128)}, f32[8,128,256]{2,1,0:T(8,128)}, u32[]{:S(2)}, u32[]{:S(2)}) collective-permute-start(f32[8,128,256]{2,1,0:T(8,128)} %collective-permute-done.4.refs_11_.refs_16_), channel_id=1, source_target_pairs={{1,0},{2,3},{5,4},{6,7},{9,8},{10,11},{13,12},{14,15},{17,16},{18,... | collective-permute-start | bytes 3145736 | tf_op jit(solution)/shard_map/ppermute | solution.py:359
  32.8 9.2 %collective-permute-start.6 = (f32[2,128,256]{2,1,0:T(8,128)S(1)}, f32[2,128,256]{2,1,0:T(8,128)S(1)}, u32[]{:S(2)}, u32[]{:S(2)}) collective-permute-start(f32[2,128,256]{2,1,0:T(8,128)S(1)} %get-tuple-element.62), channel_id=1, source_target_pairs={{0,8},{8,0},{4,12},{12,4},{1,9},{9,1},{5,13},{13,5},{2,10},{10,2},... | collective-permute-start | bytes 786440 | tf_op jit(solution)/shard_map/ppermute | solution.py:355
  35.0 8.3 %collective-permute-start.7 = (f32[2,128,256]{2,1,0:T(8,128)S(1)}, f32[2,128,256]{2,1,0:T(8,128)}, u32[]{:S(2)}, u32[]{:S(2)}) collective-permute-start(f32[2,128,256]{2,1,0:T(8,128)S(1)} %get-tuple-element.60), channel_id=1, source_target_pairs={{0,4},{4,0},{8,12},{12,8},{1,5},{5,1},{9,13},{13,9},{2,6},{6,2},{1... | collective-permute-start | bytes 786440 | tf_op jit(solution)/shard_map/ppermute | solution.py:356
  35.6 19.7 %collective-permute-start.8 = (f32[2,128,256]{2,1,0:T(8,128)}, f32[2,128,256]{2,1,0:T(8,128)}, u32[]{:S(2)}, u32[]{:S(2)}) collective-permute-start(f32[2,128,256]{2,1,0:T(8,128)} %get-tuple-element.61), channel_id=1, source_target_pairs={{0,8},{8,0},{4,12},{12,4},{1,9},{9,1},{5,13},{13,5},{2,10},{10,2},... | collective-permute-start | bytes 786440 | tf_op jit(solution)/shard_map/ppermute | solution.py:355
  42.0 1.4 %copy-start.5 = (f32[2,128,256]{2,1,0:T(8,128)}, f32[2,128,256]{2,1,0:T(8,128)S(1)}, u32[]{:S(2)}) copy-start(f32[2,128,256]{2,1,0:T(8,128)S(1)} %collective-permute-done.6.refs_6_) | copy-start | bytes 786436
  42.0 13.3 %collective-permute-start.9 = (f32[2,128,256]{2,1,0:T(8,128)}, f32[2,128,256]{2,1,0:T(8,128)}, u32[]{:S(2)}, u32[]{:S(2)}) collective-permute-start(f32[2,128,256]{2,1,0:T(8,128)} %get-tuple-element.59), channel_id=1, source_target_pairs={{0,4},{4,0},{8,12},{12,8},{1,5},{5,1},{9,13},{13,9},{2,6},{6,2},{1... | collective-permute-start | bytes 786440 | tf_op jit(solution)/shard_map/ppermute | solution.py:356
  55.3 23.5 %collective-permute-start.11 = (f32[1,1024,256]{2,1,0:T(8,128)}, f32[1,1024,256]{2,1,0:T(8,128)}, u32[]{:S(2)}, u32[]{:S(2)}) collective-permute-start(f32[1,1024,256]{2,1,0:T(8,128)} %get-tuple-element.46.refs_5_), channel_id=1, source_target_pairs={{0,16},{16,0},{1,17},{17,1},{2,18},{18,2},{3,19},{19,3},{4,20},{20... | collective-permute-start | bytes 3145736 | tf_op jit(solution)/shard_map/ppermute | solution.py:385
  55.4 23.4 %collective-permute-start.12 = (f32[1,1024,256]{2,1,0:T(8,128)}, f32[1,1024,256]{2,1,0:T(8,128)}, u32[]{:S(2)}, u32[]{:S(2)}) collective-permute-start(f32[1,1024,256]{2,1,0:T(8,128)} %get-tuple-element.47.refs_9_), channel_id=1, source_target_pairs={{0,16},{16,0},{1,17},{17,1},{2,18},{18,2},{3,19},{19,3},{4,20},{20... | collective-permute-start | bytes 3145736 | tf_op jit(solution)/shard_map/ppermute | solution.py:385
  59.0 19.8 %copy-start.2 = (f32[2,128,256]{2,1,0:T(8,128)}, f32[2,128,256]{2,1,0:T(8,128)S(1)}, u32[]{:S(2)}) copy-start(f32[2,128,256]{2,1,0:T(8,128)S(1)} %slice.25.refs_7_.refs_11_) | copy-start | bytes 786436
  59.0 24.6 %collective-permute-start.13 = (f32[6,128,256]{2,1,0:T(8,128)}, f32[6,128,256]{2,1,0:T(8,128)}, u32[]{:S(2)}, u32[]{:S(2)}) collective-permute-start(f32[6,128,256]{2,1,0:T(8,128)} %slice.24.refs_5_.refs_10_), channel_id=1, source_target_pairs={{1,0},{2,3},{5,4},{6,7},{9,8},{10,11},{13,12},{14,15},{17,16},{18,... | collective-permute-start | bytes 2359304 | tf_op jit(solution)/shard_map/ppermute | solution.py:381
  60.3 18.5 %collective-permute-start.10 = (f32[2,128,256]{2,1,0:T(8,128)S(1)}, f32[2,128,256]{2,1,0:T(8,128)}, u32[]{:S(2)}, u32[]{:S(2)}) collective-permute-start(f32[2,128,256]{2,1,0:T(8,128)S(1)} %slice.25.refs_7_.refs_11_), channel_id=1, source_target_pairs={{0,16},{16,0},{1,17},{17,1},{2,18},{18,2},{3,19},{19,3},{4,20},{20... | collective-permute-start | bytes 786440 | tf_op jit(solution)/shard_map/ppermute | solution.py:383
  60.4 30.3 %collective-permute-start.15 = (f32[2,128,256]{2,1,0:T(8,128)S(1)}, f32[2,128,256]{2,1,0:T(8,128)}, u32[]{:S(2)}, u32[]{:S(2)}) collective-permute-start(f32[2,128,256]{2,1,0:T(8,128)S(1)} %slice.25.refs_7_.refs_11_), channel_id=1, source_target_pairs={{1,0},{2,3},{5,4},{6,7},{9,8},{10,11},{13,12},{14,15},{17,16},{18,... | collective-permute-start | bytes 786440 | tf_op jit(solution)/shard_map/ppermute | solution.py:382
  83.6 7.9 %copy-start.4 = (s32[1,8,1,512]{3,2,1,0:T(1,128)S(1)}, s32[1,8,1,512]{3,2,1,0:T(1,128)}, u32[]{:S(2)}) copy-start(s32[1,8,1,512]{3,2,1,0:T(1,128)} %param.7) | copy-start | bytes 49156
  90.8 5.2 %collective-permute-start.16 = (f32[512,1024]{1,0:T(8,128)}, f32[512,1024]{1,0:T(8,128)}, u32[]{:S(2)}, u32[]{:S(2)}) collective-permute-start(f32[512,1024]{1,0:T(8,128)} %get-tuple-element.54.refs_1_), channel_id=1, source_target_pairs={{0,16},{16,0},{1,17},{17,1},{2,18},{18,2},{3,19},{19,3},{4,20},{20... | collective-permute-start | bytes 6291464 | tf_op jit(solution)/shard_map/ppermute | solution.py:426
  90.9 7.9 %collective-permute-start.14 = (f32[512,1024]{1,0:T(8,128)}, f32[512,1024]{1,0:T(8,128)}, u32[]{:S(2)}, u32[]{:S(2)}) collective-permute-start(f32[512,1024]{1,0:T(8,128)} %get-tuple-element.52.refs_0_), channel_id=1, source_target_pairs={{0,16},{16,0},{1,17},{17,1},{2,18},{18,2},{3,19},{19,3},{4,20},{20... | collective-permute-start | bytes 6291464 | tf_op jit(solution)/shard_map/ppermute | solution.py:423
  91.4 4.6 %collective-permute-start.18 = (f32[2,128,256]{2,1,0:T(8,128)}, f32[2,128,256]{2,1,0:T(8,128)S(1)}, u32[]{:S(2)}, u32[]{:S(2)}) collective-permute-start(f32[2,128,256]{2,1,0:T(8,128)} %collective-permute-done.15.refs_6_.refs_10_), channel_id=1, source_target_pairs={{0,16},{16,0},{1,17},{17,1},{2,18},{18,2},{3,19},{19,3},{4,20},{20... | collective-permute-start | bytes 786440 | tf_op jit(solution)/shard_map/ppermute | solution.py:425
  91.4 3.6 %collective-permute-start.17 = (s32[8,4,128]{2,1,0:T(4,128)S(1)}, s32[8,4,128]{2,1,0:T(4,128)S(1)}, u32[]{:S(2)}, u32[]{:S(2)}) collective-permute-start(s32[8,4,128]{2,1,0:T(4,128)S(1)} %bitcast.19), channel_id=1, source_target_pairs={{0,16},{16,0},{1,17},{17,1},{2,18},{18,2},{3,19},{19,3},{4,20},{20... | collective-permute-start | bytes 49160 | tf_op jit(solution)/shard_map/ppermute | solution.py:363
  95.1 3.7 %copy-start.6 = (s32[8,4,128]{2,1,0:T(4,128)}, s32[8,4,128]{2,1,0:T(4,128)S(1)}, u32[]{:S(2)}) copy-start(s32[8,4,128]{2,1,0:T(4,128)S(1)} %collective-permute-done.17.refs_12_.refs_16_) | copy-start | bytes 49156
  96.0 2.8 %copy-start.3 = (f32[2,128,256]{2,1,0:T(8,128)}, f32[2,128,256]{2,1,0:T(8,128)S(1)}, u32[]{:S(2)}) copy-start(f32[2,128,256]{2,1,0:T(8,128)S(1)} %collective-permute-done.18.refs_14_.refs_18_) | copy-start | bytes 786436
